TPU v7x, 32 devices: a whole 2x2x4 slice. The times are simulated.
32 devices in a mesh: row: 8 (over z, y), col: 4 (over x, core).
Axes of the slice: x: 2, y: 2, z: 4, core: 2. Of those that a mesh axis runs over, the one named last changes fastest.
Arguments:
- patches: bfloat16 [64, 64, 384], P('row', 'col'), may hold values from -10 to 10
- tissue: int32 [64, 64], P('row', 'col'), may hold values from 0 to 1
- in_weight: bfloat16 [384, 1536], replicated, may hold values from -0.3125 to 0.3125
- conv_weight: float32 [3, 3, 768], replicated, may hold values from -2 to 2
- conv_bias: float32 [768], replicated, may hold values from -3 to 3
- x_weight: bfloat16 [768, 224], replicated, may hold values from -0.21875 to 0.21875
- dt_weight: bfloat16 [4, 24, 768], replicated, may hold values from -1.25 to 1.25
- dt_bias: float32 [4, 768], replicated, may hold values from -5.5 to -3.5
- decay_rate: float32 [4, 768, 16], replicated, may hold values from 0.0001 to 4
- skip_gain: float32 [768], replicated, may hold values from 0.5 to 2
- norm_gain: float32 [768], replicated, may hold values from 0.1 to 1.9
- out_weight: bfloat16 [768, 384], replicated, may hold values from -0.21875 to 0.21875
Outputs:
- result: bfloat16 [64, 64, 384], P('row', 'col')
All inputs are finite; a program needn't handle non-finite values.
Results may differ from a plain program's by a relative error of at most 0.0076.
Values may be sent and summed in bfloat16 or wider, within the bound.
A program may use at most 256 MiB of HBM per device.

v0:
```python
import jax
import jax.numpy as jnp
from jax import lax
from jax.sharding import PartitionSpec as P


def entering(part, axis, combine, identity, reverse):
    count = lax.axis_size(axis)
    place = lax.axis_index(axis)
    ahead = count - 1 - place if reverse else place
    gathered = jax.tree.map(lambda a: lax.all_gather(a, axis), part)
    state = jax.tree.map(lambda a, e: jnp.zeros_like(a) + jnp.asarray(e, a.dtype), part, identity)

    def one(step, state):
        source = count - 1 - step if reverse else step
        return combine(
            state, jax.tree.map(lambda a: lax.dynamic_index_in_dim(a, source, 0, False), gathered)
        )

    return lax.fori_loop(0, ahead, one, state)


def spread(block, axis, holder):
    block = jnp.where(lax.axis_index(axis) == holder, block, jnp.zeros_like(block))
    return lax.psum(block, axis)


def padded(cells, sides, width):
    for axis, dim in sides:
        count = lax.axis_size(axis)
        ends = count - 1
        head = lax.slice_in_dim(cells, 0, width, axis=dim)
        tail = lax.slice_in_dim(cells, cells.shape[dim] - width, cells.shape[dim], axis=dim)
        cells = jnp.concatenate(
            [
                lax.ppermute(tail, axis, [(i, (i + 1) % count) for i in range(ends)]),
                cells,
                lax.ppermute(head, axis, [((i + 1) % count, i) for i in range(ends)]),
            ],
            axis=dim,
        )
    return cells


def make_combine(decays):

    def combine(earlier, following):
        return (
            earlier[0] + following[0],
            jnp.exp(-decays * following[0][..., None, :]) * earlier[1] + following[1],
        )

    return combine


def ordered_prefix(combine, parts, backward):
    if backward:
        parts = tuple((member[::-1] for member in parts))
    inclusive = lax.associative_scan(combine, parts)
    exclusive = tuple(
        (jnp.concatenate([jnp.zeros_like(member[:1]), member[:-1]], axis=0) for member in inclusive)
    )
    whole = tuple((member[-1] for member in inclusive))
    if backward:
        exclusive = tuple((member[::-1] for member in exclusive))
    return (exclusive, whole)


def row_chain(segment, combine, backward):
    neutral = tuple((jnp.zeros_like(member) for member in segment))
    inner_prefix = entering(segment, "col", combine, neutral, backward)
    root_index = 0 if backward else lax.axis_size("col") - 1
    whole = jax.tree.map(
        lambda part: spread(part, "col", root_index), combine(inner_prefix, segment)
    )
    local_prefix, device_total = ordered_prefix(combine, whole, backward)
    neutral_total = tuple((jnp.zeros_like(member) for member in device_total))
    outer_prefix = entering(device_total, "row", combine, neutral_total, backward)
    lifted = (outer_prefix[0][None], outer_prefix[1][None])
    return combine(combine(lifted, local_prefix), inner_prefix)


def col_chain(segment, combine, backward):
    neutral = tuple((jnp.zeros_like(member) for member in segment))
    inner_prefix = entering(segment, "row", combine, neutral, backward)
    root_index = 0 if backward else lax.axis_size("row") - 1
    whole = jax.tree.map(
        lambda part: spread(part, "row", root_index), combine(inner_prefix, segment)
    )
    local_prefix, device_total = ordered_prefix(combine, whole, backward)
    neutral_total = tuple((jnp.zeros_like(member) for member in device_total))
    outer_prefix = entering(device_total, "col", combine, neutral_total, backward)
    lifted = (outer_prefix[0][None], outer_prefix[1][None])
    return combine(combine(lifted, local_prefix), inner_prefix)


def local_layout(values, columns_first, backward):
    arranged = values if columns_first else jnp.transpose(values, (1, 0, 2))
    if backward:
        arranged = arranged[::-1]
    return arranged


def tile_layout(arranged, columns_first, backward):
    if backward:
        arranged = arranged[::-1]
    return arranged if columns_first else jnp.transpose(arranged, (1, 0, 2))


def segment_totals(steps_dt, inputs_du, b_coeffs, decays):

    def advance(carried, inputs):
        delta, driven, b_row = inputs
        sums, states = carried
        states = (
            jnp.exp(-decays * delta[:, None, :]) * states + driven[:, None, :] * b_row[:, :, None]
        )
        return ((sums + delta, states), None)

    width_seg = steps_dt.shape[1]
    start = (
        jnp.zeros((width_seg, decays.shape[1]), jnp.float32),
        jnp.zeros((width_seg,) + decays.shape, jnp.float32),
    )
    totals, unused = lax.scan(advance, start, (steps_dt, inputs_du, b_coeffs))
    return totals


def segment_outputs(entry, steps_dt, inputs_du, b_coeffs, c_coeffs, decays):

    def advance(states, inputs):
        delta, driven, b_row, c_row = inputs
        states = (
            jnp.exp(-decays * delta[:, None, :]) * states + driven[:, None, :] * b_row[:, :, None]
        )
        return (states, jnp.sum(states * c_row[:, :, None], axis=1))

    final_states, outputs = lax.scan(advance, entry, (steps_dt, inputs_du, b_coeffs, c_coeffs))
    return outputs


def per_device(
    patches,
    tissue,
    in_weight,
    conv_weight,
    conv_bias,
    x_weight,
    dt_weight,
    dt_bias,
    decay_rate,
    skip_gain,
    norm_gain,
    out_weight,
):
    tile_rows, tile_cols, channels = patches.shape
    inner_width = out_weight.shape[0]
    state_width = decay_rate.shape[2]
    rank_width = dt_weight.shape[1]
    token_count = tile_rows * tile_cols
    flattened = patches.reshape(token_count, channels)
    projected = jnp.dot(flattened, in_weight, preferred_element_type=jnp.float32)
    x_inner = (
        projected[:, :inner_width].astype(jnp.bfloat16).reshape(tile_rows, tile_cols, inner_width)
    )
    gate_half = projected[:, inner_width:].astype(jnp.bfloat16)
    framed = padded(x_inner, (("row", 0), ("col", 1)), 1).astype(jnp.float32)
    conv_sum = jnp.zeros((tile_rows, tile_cols, inner_width), jnp.float32) + conv_bias
    for offset_row in range(3):
        for offset_col in range(3):
            conv_sum = (
                conv_sum
                + framed[offset_row : offset_row + tile_rows, offset_col : offset_col + tile_cols]
                * conv_weight[offset_row, offset_col]
            )
    activated = jax.nn.silu(conv_sum).astype(jnp.bfloat16).reshape(token_count, inner_width)
    scan_proj = jnp.dot(activated, x_weight, preferred_element_type=jnp.float32)
    tissue_live = tissue.reshape(token_count, 1).astype(jnp.float32)
    activated_wide = activated.astype(jnp.float32)
    width_each = rank_width + 2 * state_width
    combined = jnp.zeros((token_count, inner_width), jnp.float32)
    for direction in range(4):
        section = scan_proj[:, direction * width_each : (direction + 1) * width_each]
        low_rank = section[:, :rank_width].astype(jnp.bfloat16)
        steps_dt = (
            jax.nn.softplus(
                jnp.dot(low_rank, dt_weight[direction], preferred_element_type=jnp.float32)
                + dt_bias[direction]
            )
            * tissue_live
        )
        inputs_du = steps_dt * activated_wide
        b_coeffs = section[:, rank_width : rank_width + state_width]
        c_coeffs = section[:, rank_width + state_width :]
        columns_first = direction >= 2
        backward = direction % 2 == 1
        layout = [
            local_layout(member.reshape(tile_rows, tile_cols, -1), columns_first, backward)
            for member in (steps_dt, inputs_du, b_coeffs, c_coeffs)
        ]
        decays = jnp.transpose(decay_rate[direction], (1, 0))
        combine = make_combine(decays)
        segment = segment_totals(layout[0], layout[1], layout[2], decays)
        if columns_first:
            entry = col_chain(segment, combine, backward)
        else:
            entry = row_chain(segment, combine, backward)
        outputs = segment_outputs(entry[1], layout[0], layout[1], layout[2], layout[3], decays)
        combined = combined + tile_layout(outputs, columns_first, backward).reshape(
            token_count, inner_width
        )
    combined = combined + skip_gain * activated_wide
    mean_value = jnp.mean(combined, axis=1, keepdims=True)
    centered = combined - mean_value
    variance = jnp.mean(centered * centered, axis=1, keepdims=True)
    normed = centered * lax.rsqrt(variance + 1e-05) * norm_gain
    mixed = (normed * jax.nn.silu(gate_half.astype(jnp.float32))).astype(jnp.bfloat16)
    result = jnp.dot(mixed, out_weight, preferred_element_type=jnp.float32) * tissue_live
    return result.astype(jnp.bfloat16).reshape(tile_rows, tile_cols, channels)


def solution(mesh):
    in_specs = (
        P("row", "col", None),
        P("row", "col"),
        P(),
        P(),
        P(),
        P(),
        P(),
        P(),
        P(),
        P(),
        P(),
        P(),
    )
    out_specs = P("row", "col", None)
    return jax.shard_map(
        per_device, mesh=mesh, in_specs=in_specs, out_specs=out_specs, check_vma=False
    )
```

profile of v0, /device:TPU:24, one launch (start us, length us, event | category | flops | bytes accessed | tf_op | source)
XLA Modules:
  0.0 833.1 jit_solution(831726790820794487)
XLA Ops:
  10.0 3.6 collective-permute-start
  13.5 3.3 collective-permute-start.1
  22.1 3.3 collective-permute-done.3
  34.1 14.6 %while.241 = (s32[]{:T(128)}, f32[8,768]{1,0:T(8,128)S(1)}, f32[8,16,768]{2,1,0:T(8,128)S(1)}, f32[16,8,768]{2,1,0:T(8,128)S(1)}, f32[1,16,768]{2,1,0:T(8,128)S(...) while((s32[]{:T(128)}, f32[8,768]{1,0:T(8,128)S(1)}, ...), condition=%wide.region_12.13_spmd.clone, body=%wide.region_11.12_spmd.clone.sunk | while | flops 503811 | bytes 1033844 | solution.py:125
  50.1 3.1 while.240
  54.9 6.6 all-gather.2
  61.5 6.3 all-gather
  67.7 4.2 all-gather.19.cloned.1.call-done
  72.0 3.8 while.231
  75.8 17.3 %all-gather.17.cloned.1.call-done = f32[32,16,768]{2,1,0:T(8,128)} async-done(((f32[8,16,768]{2,1,0:T(8,128)}), f32[32,16,768]{2,1,0:T(8,128)}) %all-gather.17.cloned.1.call-update) | async-done | bytes 1572880 | tf_op jit(solution)/shard_map/all_gather | solution.py:11
  96.1 21.0 %while.242 = (s32[]{:T(128)}, f32[16,768]{1,0:T(8,128)S(1)}, f32[16,16,768]{2,1,0:T(8,128)S(1)}, f32[8,16,768]{2,1,0:T(8,128)}, f32[1,16,768]{2,1,0:T(8,128)S(1)...) while((s32[]{:T(128)}, f32[16,768]{1,0:T(8,128)S(1)}, ...), condition=%wide.region_23.24_spmd.clone, body=%wide.region_22.23_spmd.clone.sunk | while | flops 1007619 | bytes 2018420 | solution.py:125
  120.3 2.9 while.243
  127.3 29.6 %all-gather.4 = f32[128,768]{1,0:T(8,128)S(1)} all-gather(f32[16,768]{1,0:T(8,128)S(1)} %get-tuple-element.1479), channel_id=6, replica_groups=mesh['row'=8,'col'=4] {'row'}, dimensions={0}, use_global_device_ids=true | all-gather | bytes 442368 | tf_op jit(solution)/shard_map/all_gather | solution.py:11
  156.9 34.3 %all-gather.6 = f32[128,768]{1,0:T(8,128)} all-gather(f32[16,768]{1,0:T(8,128)S(1)} %get-tuple-element.1485), channel_id=8, replica_groups=mesh['row'=8,'col'=4] {'row'}, dimensions={0}, use_global_device_ids=true | all-gather | bytes 442368 | tf_op jit(solution)/shard_map/all_gather | solution.py:11
  191.2 13.0 %all-reduce.66 = (f32[8,768]{1,0:T(8,128)S(1)}, f32[8,768]{1,0:T(8,128)S(1)}) all-reduce(f32[8,768]{1,0:T(8,128)S(1)} %add_select_fusion.7, f32[8,768]{1,0:T(8,128)S(1)} %add_select_fusion.6), channel_id=1, replica_groups=mesh['row'=8,'col'=4] {'col'}, use_global_device_ids=true, to_apply=%region_4.5 | all-reduce | flops 12288 | bytes 98304 | tf_op jit(solution)/shard_map/psum | solution.py:25
  220.2 7.6 all-gather.21.cloned.1.call-done
  227.9 10.0 %while.234 = (s32[]{:T(128)}, f32[16,768]{1,0:T(8,128)S(1)}, f32[16,16,768]{2,1,0:T(8,128)S(1)}, s32[]{:T(128)}, f32[8,16,768]{2,1,0:T(8,128)S(1)}, /*index=5*/f...) while((s32[]{:T(128)}, f32[16,768]{1,0:T(8,128)S(1)}, ...), condition=%wide.region_25.26_spmd, body=%wide.region_24.25_spmd.sunk | while | flops 602117 | bytes 2654351 | solution.py:20
  237.9 90.2 %all-gather.23.cloned.1.call-done = f32[128,16,768]{2,1,0:T(8,128)} async-done(((f32[16,16,768]{2,1,0:T(8,128)}), f32[128,16,768]{2,1,0:T(8,128)}) %all-gather.23.cloned.1.call-update) | async-done | bytes 6291472 | tf_op jit(solution)/shard_map/all_gather | solution.py:11
  328.7 3.1 while.237
  335.1 2.2 add_select_fusion
  338.4 82.5 %all-reduce.72.cloned.1.call-done = (f32[16,768]{1,0:T(8,128)}, f32[16,768]{1,0:T(8,128)}) async-done(((f32[16,768]{1,0:T(8,128)}, f32[16,768]{1,0:T(8,128)}), (f32[16,768]{1,0:T(8,128)}, f32[16,768]{1,0:T(8,128)})) %all-reduce.72.cloned.1.call-update) | async-done | bytes 98320 | tf_op jit(solution)/shard_map/psum | solution.py:25
  430.9 28.8 %all-gather.9 = f32[8,1,768]{2,1,0:T(1,128)S(1)} all-gather(f32[1,1,768]{2,1,0:T(1,128)S(1)} %get-tuple-element.1970), channel_id=1, replica_groups=mesh['row'=8,'col'=4] {'row'}, dimensions={0}, use_global_device_ids=true | all-gather | bytes 27648 | tf_op jit(solution)/shard_map/all_gather | solution.py:11
  460.3 30.3 %all-gather.8 = f32[8,1,768]{2,1,0:T(1,128)S(1)} all-gather(f32[1,1,768]{2,1,0:T(1,128)S(1)} %get-tuple-element.1971), channel_id=1, replica_groups=mesh['row'=8,'col'=4] {'row'}, dimensions={0}, use_global_device_ids=true | all-gather | bytes 27648 | tf_op jit(solution)/shard_map/all_gather | solution.py:11
  491.3 5.2 all-gather.10
  499.1 5.1 all-gather.11
  505.5 6.8 all-reduce.74.cloned.1.call-done
  519.7 2.1 pad.193
  528.9 2.1 pad.218
  533.7 3.6 pad.221
  554.3 2.0 pad.206
  557.2 31.9 %all_gather.83 = f32[8,16,768]{2,1,0:T(8,128)} all-gather(f32[1,16,768]{2,1,0:T(8,128)S(1)} %slice_add_fusion.14), channel_id=1, replica_groups=mesh['row'=8,'col'=4] {'row'}, dimensions={0}, use_global_device_ids=true | all-gather | bytes 442368 | tf_op jit(solution)/shard_map/all_gather | solution.py:11
  590.7 2.0 pad.308
  594.1 29.7 %while.233 = (s32[]{:T(128)}, f32[8,16,768]{2,1,0:T(8,128)S(1)}, f32[16,8,768]{2,0,1:T(8,128)S(1)}, f32[1,16,768]{2,1,0:T(8,128)S(1)}, f32[16,8,768]{2,1,0:T(8,1...) while((s32[]{:T(128)}, f32[8,16,768]{2,1,0:T(8,128)S(1)}, ...), condition=%wide.region_21.22_spmd, body=%wide.region_19.21_spmd.sunk | while | flops 583682 | bytes 1109105 | solution.py:138
  628.6 43.0 %all_gather.77 = f32[8,16,768]{2,1,0:T(8,128)} all-gather(f32[1,16,768]{2,1,0:T(8,128)S(1)} %slice_add_fusion.16), channel_id=1, replica_groups=mesh['row'=8,'col'=4] {'row'}, dimensions={0}, use_global_device_ids=true | all-gather | bytes 442368 | tf_op jit(solution)/shard_map/all_gather | solution.py:11
  671.6 9.7 %while.229 = (s32[]{:T(128)}, f32[16,768]{1,0:T(8,128)S(1)}, s32[]{:T(128)}, f32[8,768]{1,0:T(8,128)}, f32[16,768]{1,0:T(8,128)S(1)}, /*index=5*/f32[8,16,768]{2,1,0:T(8,128)}, s32[]{:T(128)}, s32[]{:T(128)}, s32[]{:T(128)}) while((s32[]{:T(128)}, f32[16,768]{1,0:T(8,128)S(1)}, s32[]{:T(128)}, f32[8,768]{1,0:T(8,128)}, ...), condition=%wide.region_7.8_spmd, body=%wide.region_6.7_spmd.sunk | while | flops 36869 | bytes 205959 | solution.py:20
  681.3 2.0 pad.304
  686.0 54.3 %while.230 = (s32[]{:T(128)}, f32[8,16,768]{2,1,0:T(8,128)S(1)}, f32[16,8,768]{2,0,1:T(8,128)}, f32[1,16,768]{2,1,0:T(8,128)S(1)}, f32[16,8,768]{2,1,0:T(8,128)}...) while((s32[]{:T(128)}, f32[8,16,768]{2,1,0:T(8,128)S(1)}, ...), condition=%wide.region_10.11_spmd, body=%wide.region_8.10_spmd.sunk | while | flops 583682 | bytes 1109105 | solution.py:138
  740.4 3.4 pad.459
  744.8 3.4 pad.222
  749.0 5.6 all_gather.89
  754.6 3.4 pad.312
  760.2 16.7 %while.236 = (s32[]{:T(128)}, f32[16,16,768]{2,1,0:T(8,128)S(1)}, f32[8,16,768]{2,1,0:T(8,128)S(1)}, f32[1,16,768]{2,1,0:T(8,128)S(1)}, f32[8,16,768]{2,1,0:T(8,...) while((s32[]{:T(128)}, f32[16,16,768]{2,1,0:T(8,128)S(1)}, ...), condition=%wide.region_32.33_spmd, body=%wide.region_30.32_spmd.sunk | while | flops 1167362 | bytes 2070633 | solution.py:138
  780.3 3.3 pad.462
  784.5 3.4 pad.238
  788.7 7.7 all_gather.95
  796.4 2.3 while.238
  798.7 3.4 pad.316
  804.6 16.8 %while.239 = (s32[]{:T(128)}, f32[16,16,768]{2,1,0:T(8,128)S(1)}, f32[8,16,768]{2,1,0:T(8,128)S(1)}, f32[1,16,768]{2,1,0:T(8,128)S(1)}, f32[8,16,768]{2,1,0:T(8,...) while((s32[]{:T(128)}, f32[16,16,768]{2,1,0:T(8,128)S(1)}, ...), condition=%wide.region_43.44_spmd, body=%wide.region_41.43_spmd.sunk | while | flops 1167362 | bytes 2070633 | solution.py:138
  (1050 shorter events, 311.1 us)
Async XLA Ops:
  7.4 64.5 %all-gather.19.cloned.1.call-start = ((), (), s32[]{:S(2)}) async-start(), calls=%async_computation.1 | async-start | bytes 1966080 | tf_op jit(solution)/shard_map/all_gather | solution.py:11
  9.9 15.6 %copy-start.123 = (f32[768]{0:T(1024)S(1)}, f32[768]{0:T(1024)}, u32[]{:S(2)}) copy-start(f32[768]{0:T(1024)} %param.48) | copy-start | bytes 9220
  10.0 7.7 collective-permute-start
  13.5 5.7 collective-permute-start.1
  17.5 201.2 %copy-start.22 = (f32[16,768]{1,0:T(8,128)}, f32[16,768]{1,0:T(8,128)S(1)}, u32[]{:S(2)}) copy-start(f32[16,768]{1,0:T(8,128)S(1)} %get-tuple-element.3112) | copy-start | bytes 147460
  17.5 202.0 %copy-start.24 = (f32[16,768]{1,0:T(8,128)}, f32[16,768]{1,0:T(8,128)S(1)}, u32[]{:S(2)}) copy-start(f32[16,768]{1,0:T(8,128)S(1)} %get-tuple-element.3169) | copy-start | bytes 147460
  19.3 2.8 collective-permute-start.2
  20.6 4.8 collective-permute-start.3
  49.4 43.8 %all-gather.17.cloned.1.call-start = ((), (), s32[]{:S(2)}) async-start(), calls=%async_computation | async-start | bytes 1966080 | tf_op jit(solution)/shard_map/all_gather | solution.py:11
  53.3 18.6 %copy-start.62 = (f32[16,8,768]{2,1,0:T(8,128)}, f32[16,8,768]{2,1,0:T(8,128)S(1)}, u32[]{:S(2)}) copy-start(f32[16,8,768]{2,1,0:T(8,128)S(1)} %get-tuple-element.3278) | copy-start | bytes 1179652
  53.3 18.7 %copy-start.63 = (f32[16,8,768]{2,1,0:T(8,128)}, f32[16,8,768]{2,1,0:T(8,128)S(1)}, u32[]{:S(2)}) copy-start(f32[16,8,768]{2,1,0:T(8,128)S(1)} %get-tuple-element.3279) | copy-start | bytes 1179652
  54.0 158.1 %all-reduce.76.cloned.1.call-start = ((), (), s32[]{:S(2)}) async-start(), calls=%async_computation.6 | async-start | bytes 1572864 | tf_op jit(solution)/shard_map/psum | solution.py:25
  75.8 17.4 %copy-start.54 = (f32[8,768]{1,0:T(8,128)}, f32[8,768]{1,0:T(8,128)S(1)}, u32[]{:S(2)}) copy-start(f32[8,768]{1,0:T(8,128)S(1)} %get-tuple-element.1475) | copy-start | bytes 73732
  75.8 17.4 %copy-start.15 = (f32[1,16,768]{2,1,0:T(8,128)}, f32[1,16,768]{2,1,0:T(8,128)S(1)}, u32[]{:S(2)}) copy-start(f32[1,16,768]{2,1,0:T(8,128)S(1)} %get-tuple-element.3256) | copy-start | bytes 147460
  96.0 131.7 %all-gather.21.cloned.1.call-start = ((), (), s32[]{:S(2)}) async-start(), calls=%async_computation.2 | async-start | bytes 7077888 | tf_op jit(solution)/shard_map/all_gather | solution.py:11
  118.0 210.0 %all-gather.23.cloned.1.call-start = ((), (), s32[]{:S(2)}) async-start(), calls=%async_computation.3 | async-start | bytes 7077888 | tf_op jit(solution)/shard_map/all_gather | solution.py:11
  123.2 82.5 %copy-start.30 = (f32[16,768]{1,0:T(8,128)}, f32[16,768]{1,0:T(8,128)S(1)}, u32[]{:S(2)}) copy-start(f32[16,768]{1,0:T(8,128)S(1)} %get-tuple-element.1485) | copy-start | bytes 147460
  123.3 82.5 %copy-start.37 = (f32[8,16,768]{2,1,0:T(8,128)}, f32[8,16,768]{2,1,0:T(8,128)S(1)}, u32[]{:S(2)}) copy-start(f32[8,16,768]{2,1,0:T(8,128)S(1)} %get-tuple-element.3270) | copy-start | bytes 1179652
  123.3 82.5 %copy-start.38 = (f32[8,16,768]{2,1,0:T(8,128)}, f32[8,16,768]{2,1,0:T(8,128)S(1)}, u32[]{:S(2)}) copy-start(f32[8,16,768]{2,1,0:T(8,128)S(1)} %get-tuple-element.3271) | copy-start | bytes 1179652
  123.3 82.4 %copy-start.80 = (f32[8,16,16]{2,1,0:T(8,128)}, f32[8,16,16]{2,1,0:T(8,128)S(1)}, u32[]{:S(2)}) copy-start(f32[8,16,16]{2,1,0:T(8,128)S(1)} %get-tuple-element.3286) | copy-start | bytes 24580
  123.3 67.9 %copy-start.55 = (f32[8,768]{1,0:T(8,128)S(1)}, f32[8,768]{1,0:T(8,128)}, u32[]{:S(2)}) copy-start(f32[8,768]{1,0:T(8,128)} %copy-done.54) | copy-start | bytes 73732
  123.3 67.9 %copy-start.49 = (f32[8,768]{1,0:T(8,128)S(1)}, f32[8,768]{1,0:T(8,128)}, u32[]{:S(2)}) copy-start(f32[8,768]{1,0:T(8,128)} %copy-done.48) | copy-start | bytes 73732
  124.2 296.7 %all-reduce.72.cloned.1.call-start = ((), (), s32[]{:S(2)}) async-start(), calls=%async_computation.4 | async-start | bytes 196608 | tf_op jit(solution)/shard_map/psum | solution.py:25
  237.9 90.9 %copy-start.11 = (f32[1,16,768]{2,1,0:T(8,128)}, f32[1,16,768]{2,1,0:T(8,128)S(1)}, u32[]{:S(2)}) copy-start(f32[1,16,768]{2,1,0:T(8,128)S(1)} %get-tuple-element.3252) | copy-start | bytes 147460
  237.9 90.9 %copy-start.31 = (f32[16,768]{1,0:T(8,128)}, f32[16,768]{1,0:T(8,128)S(1)}, u32[]{:S(2)}) copy-start(f32[16,768]{1,0:T(8,128)S(1)} %get-tuple-element.1481) | copy-start | bytes 147460
  334.8 177.5 %all-reduce.74.cloned.1.call-start = ((), (), s32[]{:S(2)}) async-start(), calls=%async_computation.5 | async-start | bytes 3145728 | tf_op jit(solution)/shard_map/psum | solution.py:25
  422.6 89.7 %copy-start.20 = (f32[16,768]{1,0:T(8,128)S(1)}, f32[16,768]{1,0:T(8,128)}, u32[]{:S(2)}) copy-start(f32[16,768]{1,0:T(8,128)} %get-tuple-element.3058) | copy-start | bytes 147460
  426.5 64.1 %copy-start.96 = (f32[3,768]{1,0:T(4,128)}, f32[3,768]{1,0:T(4,128)S(1)}, u32[]{:S(2)}) copy-start(f32[3,768]{1,0:T(4,128)S(1)} %slice.760) | copy-start | bytes 27652
  427.4 86.2 %copy-start.83 = (f32[7,768]{1,0:T(8,128)}, f32[7,768]{1,0:T(8,128)S(1)}, u32[]{:S(2)}) copy-start(f32[7,768]{1,0:T(8,128)S(1)} %slice.762) | copy-start | bytes 64516
  497.2 16.6 %copy-start.81 = (f32[7,768]{1,0:T(8,128)}, f32[7,768]{1,0:T(8,128)S(1)}, u32[]{:S(2)}) copy-start(f32[7,768]{1,0:T(8,128)S(1)} %slice.809) | copy-start | bytes 64516
  628.6 55.8 %copy-start.6 = (f32[8,16,768]{2,1,0:T(8,128)S(1)}, f32[8,16,768]{2,1,0:T(8,128)}, u32[]{:S(2)}) copy-start(f32[8,16,768]{2,1,0:T(8,128)} %copy-done.5) | copy-start | bytes 1179652
  686.0 54.3 %copy-start.47 = (f32[8,16,768]{2,1,0:T(8,128)S(1)}, f32[8,16,768]{2,1,0:T(8,128)}, u32[]{:S(2)}) copy-start(f32[8,16,768]{2,1,0:T(8,128)} %add.934) | copy-start | bytes 1179652
  686.0 57.7 %copy-start.84 = (f32[1,16,768]{2,1,0:T(8,128)S(1)}, f32[1,16,768]{2,1,0:T(8,128)}, u32[]{:S(2)}) copy-start(f32[1,16,768]{2,1,0:T(8,128)} %slice.914) | copy-start | bytes 147460
  760.2 17.5 %slice-start = ((f32[8,16,768]{2,1,0:T(8,128)}), f32[1,16,768]{2,1,0:T(8,128)S(1)}, s32[]{:S(2)}) async-start(f32[8,16,768]{2,1,0:T(8,128)} %copy-done.33), calls=%async_computation.7 | async-start | bytes 98304 | tf_op jit(solution)/shard_map/slice | solution.py:59
  760.2 17.5 %copy-start.69 = (f32[3,16,768]{2,1,0:T(8,128)S(1)}, f32[3,16,768]{2,1,0:T(8,128)}, u32[]{:S(2)}) copy-start(f32[3,16,768]{2,1,0:T(8,128)} %fusion.31) | copy-start | bytes 442372
  804.5 16.9 %copy-start.50 = (f32[16,8,768]{2,0,1:T(8,128)S(1)}, f32[16,8,768]{2,0,1:T(8,128)}, u32[]{:S(2)}) copy-start(f32[16,8,768]{2,0,1:T(8,128)} %rev.52) | copy-start | bytes 1179652
  804.5 16.9 %copy-start.51 = (f32[16,8,768]{2,0,1:T(8,128)S(1)}, f32[16,8,768]{2,0,1:T(8,128)}, u32[]{:S(2)}) copy-start(f32[16,8,768]{2,0,1:T(8,128)} %get-tuple-element.1472) | copy-start | bytes 1179652
  804.5 16.9 %copy-start.53 = (f32[8,16,768]{2,1,0:T(8,128)S(1)}, f32[8,16,768]{2,1,0:T(8,128)}, u32[]{:S(2)}) copy-start(f32[8,16,768]{2,1,0:T(8,128)} %copy-done.52) | copy-start | bytes 1179652
  804.5 16.9 %copy-start.99 = (f32[768]{0:T(1024)S(1)}, f32[768]{0:T(1024)}, u32[]{:S(2)}) copy-start(f32[768]{0:T(1024)} %copy-done.98) | copy-start | bytes 9220
  804.5 16.9 %copy-start.101 = (f32[768]{0:T(1024)S(1)}, f32[768]{0:T(1024)}, u32[]{:S(2)}) copy-start(f32[768]{0:T(1024)} %copy-done.100) | copy-start | bytes 9220
  804.6 16.9 %copy-start.103 = (f32[768]{0:T(1024)S(1)}, f32[768]{0:T(1024)}, u32[]{:S(2)}) copy-start(f32[768]{0:T(1024)} %copy-done.102) | copy-start | bytes 9220
  804.6 16.9 %copy-start.105 = (f32[768]{0:T(1024)S(1)}, f32[768]{0:T(1024)}, u32[]{:S(2)}) copy-start(f32[768]{0:T(1024)} %copy-done.104) | copy-start | bytes 9220
  804.6 16.9 %copy-start.108 = (f32[768]{0:T(1024)S(1)}, f32[768]{0:T(1024)}, u32[]{:S(2)}) copy-start(f32[768]{0:T(1024)} %copy-done.107) | copy-start | bytes 9220
  804.6 16.9 %copy-start.111 = (f32[768]{0:T(1024)S(1)}, f32[768]{0:T(1024)}, u32[]{:S(2)}) copy-start(f32[768]{0:T(1024)} %copy-done.110) | copy-start | bytes 9220
  804.6 16.9 %copy-start.114 = (f32[768]{0:T(1024)S(1)}, f32[768]{0:T(1024)}, u32[]{:S(2)}) copy-start(f32[768]{0:T(1024)} %copy-done.113) | copy-start | bytes 9220
  804.6 16.9 %copy-start.117 = (f32[768]{0:T(1024)S(1)}, f32[768]{0:T(1024)}, u32[]{:S(2)}) copy-start(f32[768]{0:T(1024)} %copy-done.116) | copy-start | bytes 9220
  804.6 16.9 %copy-start.124 = (f32[768]{0:T(1024)S(1)}, f32[768]{0:T(1024)}, u32[]{:S(2)}) copy-start(f32[768]{0:T(1024)} %param.48) | copy-start | bytes 9220
  804.6 16.9 %copy-start.126 = (f32[768]{0:T(1024)S(1)}, f32[768]{0:T(1024)}, u32[]{:S(2)}) copy-start(f32[768]{0:T(1024)} %param.53) | copy-start | bytes 9220
  (112 other events, 483.6 us)
Sparse Core Ops, SparseCore 0:
  49.5 22.3 all-gather.18
  73.5 19.6 all-gather.16
  96.1 39.6 all-reduce.75
Sparse Core Ops, SparseCore 1:
  118.1 109.6 all-gather.20
  229.8 98.1 all-gather.22
  334.9 86.0 all-reduce.71
  424.5 87.7 all-reduce.73
where the time goes:
time: 845 us; the launch traced here: 833 us
  blocking collectives  247 us (29%)
  local copies, waits for them, and re-layouts  228 us (27%)
  waiting for transfers between devices  214 us (25%)
  other arithmetic  106 us (13%)
  between operations  17.6 us (2%)
  starting transfers between devices  9.93 us (1%)
    all_gather x12, blocking collectives, entering(): gathered = jax.tree.map(lambda a: lax.all_gather(a, axis), part)  234 us
    all_gather x4, waiting for transfers between devices, entering(): gathered = jax.tree.map(lambda a: lax.all_gather(a, axis), part)  119 us
    psum x3, waiting for transfers between devices, spread(): return lax.psum(block, axis)  89.3 us
    mul x144, local copies, waits for them, and re-layouts, advance(): driven[:, None, :] * b_row[:, :, None]  62.5 us
    add x39, other arithmetic, combine(): jnp.exp(-decays * following[0][..., None, :]) * earlier[1] + following[1]  34.4 us
    mul x48, local copies, waits for them, and re-layouts, advance(): return (states, jnp.sum(states * c_row[:, :, None], axis=1))  33.5 us
    dynamic_update_slice x80, local copies, waits for them, and re-layouts, segment_outputs(): lax.scan(advance, entry, (steps_dt, inputs_du, b_coeffs, c_coeffs))  30.7 us
    unnamed x307, local copies, waits for them, and re-layouts  25.8 us
  transfers between devices with their start and end apart: 11, of which 8 were waited for; matrix products, arithmetic and copies ran while one was open for 10% of the time, Pallas kernels for 0%

commit v1 on v0

v1 whole, which is shorter than its diff:
```python
import functools
import math
import jax
import jax.numpy as jnp
from jax import lax
from jax.experimental import pallas as pl
from jax.experimental.pallas import tpu as pltpu
from jax.sharding import PartitionSpec as P

MESH = pl.DeviceIdType.MESH
VMEM = pl.BlockSpec(memory_space=pltpu.VMEM)
ANY = pl.BlockSpec(memory_space=pl.ANY)
LIMIT = 56 * 1024 * 1024
LOG2E = math.log2(math.e)
AROUND = ((-1, 0), (1, 0), (0, -1), (0, 1), (-1, -1), (-1, 1), (1, -1), (1, 1))


def lanes(width):
    return -(-width // 128) * 128


def halo_kernel(nr, nc, strips, out, send, recv):
    r, c = lax.axis_index("row"), lax.axis_index("col")
    peers = [(lax.rem(r + dr + nr, nr), lax.rem(c + dc + nc, nc)) for dr, dc in AROUND]
    barrier = pltpu.get_barrier_semaphore()
    for peer in peers:
        pl.semaphore_signal(barrier, inc=1, device_id=peer, device_id_type=MESH)
    pl.semaphore_wait(barrier, len(peers))
    copies = []
    for d, peer in enumerate(peers):
        copy = pltpu.make_async_remote_copy(
            src_ref=strips.at[d], dst_ref=out.at[d], send_sem=send.at[d], recv_sem=recv.at[d],
            device_id=peer, device_id_type=MESH)
        copy.start()
        copies.append(copy)
    for copy in copies:
        copy.wait()


def halo(strips, nr, nc):
    return pl.pallas_call(
        functools.partial(halo_kernel, nr, nc),
        out_shape=jax.ShapeDtypeStruct(strips.shape, strips.dtype),
        in_specs=[VMEM], out_specs=VMEM,
        scratch_shapes=[pltpu.SemaphoreType.DMA((8,)), pltpu.SemaphoreType.DMA((8,))],
        compiler_params=pltpu.CompilerParams(collective_id=0, has_side_effects=True),
        name="halo",
    )(strips)


def greet(sizes):
    barrier = pltpu.get_barrier_semaphore()
    for axis, n in sizes:
        me = lax.axis_index(axis)
        for k in range(1, n):
            pl.semaphore_signal(barrier, inc=1, device_id={axis: lax.rem(me + k, n)},
                                device_id_type=MESH)
    pl.semaphore_wait(barrier, sum(n - 1 for axis, n in sizes))


def swap_kernel(sizes, *refs):
    count = len(sizes)
    ins, outs, sems = refs[:count], refs[count:2 * count], refs[2 * count:]
    greet(sizes)
    copies = []
    for place, (axis, n) in enumerate(sizes):
        send, recv, own = sems[3 * place:3 * place + 3]
        me = lax.axis_index(axis)
        for k in range(1, n):
            to = lax.rem(me + k, n)
            copies.append(pltpu.make_async_remote_copy(
                src_ref=ins[place].at[to], dst_ref=outs[place].at[me],
                send_sem=send.at[k], recv_sem=recv.at[k],
                device_id={axis: to}, device_id_type=MESH))
        copies.append(pltpu.make_async_copy(ins[place].at[me], outs[place].at[me], own.at[0]))
    for copy in copies:
        copy.start()
    for copy in copies:
        copy.wait()


def swap(sizes, arrays, collective_id):
    scratch = []
    for axis, n in sizes:
        scratch += [pltpu.SemaphoreType.DMA((n,)), pltpu.SemaphoreType.DMA((n,)),
                    pltpu.SemaphoreType.DMA((1,))]
    return pl.pallas_call(
        functools.partial(swap_kernel, sizes),
        out_shape=[jax.ShapeDtypeStruct(a.shape, a.dtype) for a in arrays],
        in_specs=[ANY] * len(arrays), out_specs=[ANY] * len(arrays),
        scratch_shapes=scratch,
        compiler_params=pltpu.CompilerParams(collective_id=collective_id, has_side_effects=True),
        name="swap%d" % collective_id,
    )(*arrays)


def turn(rows, cols):
    count = rows * cols
    out = lax.broadcasted_iota(jnp.int32, (count, count), 0)
    src = lax.broadcasted_iota(jnp.int32, (count, count), 1)
    return (lax.rem(out, rows) * cols + lax.div(out, rows) == src).astype(jnp.float32).astype(jnp.bfloat16)


def turn_back(rows, cols):
    count = rows * cols
    out = lax.broadcasted_iota(jnp.int32, (count, count), 0)
    src = lax.broadcasted_iota(jnp.int32, (count, count), 1)
    return (lax.rem(out, cols) * rows + lax.div(out, cols) == src).astype(jnp.float32).astype(jnp.bfloat16)


def dot(a, b):
    return jnp.dot(a, b, preferred_element_type=jnp.float32)


def front_kernel(dims, patches, strips, live, w_in, w_conv, bias, w_x, tissue,
                 msg_row, msg_col, act_out, gate_out, frame):
    rows, cols, inner, nr, nc = dims
    tokens = rows * cols
    projected = dot(patches[...], w_in[...])
    gate_out[...] = projected[:, inner:].astype(jnp.bfloat16)
    body = projected[:, :inner].astype(jnp.bfloat16).astype(jnp.float32)
    rim = dot(strips[...], w_in[:, :inner]).astype(jnp.bfloat16).astype(jnp.float32) * live[...]
    frame[1:rows + 1, 1:cols + 1, :] = body.reshape(rows, cols, inner)
    frame[rows + 1, 1:cols + 1, :] = rim[0:cols]
    frame[0, 1:cols + 1, :] = rim[cols:2 * cols]
    for i in range(rows):
        frame[i + 1, cols + 1:cols + 2, :] = rim[2 * cols + i:2 * cols + i + 1]
        frame[i + 1, 0:1, :] = rim[3 * cols + i:3 * cols + i + 1]
    frame[rows + 1, cols + 1:cols + 2, :] = rim[4 * cols:4 * cols + 1]
    frame[rows + 1, 0:1, :] = rim[5 * cols:5 * cols + 1]
    frame[0, cols + 1:cols + 2, :] = rim[6 * cols:6 * cols + 1]
    frame[0, 0:1, :] = rim[7 * cols:7 * cols + 1]
    total = jnp.zeros((rows, cols, inner), jnp.float32) + bias[...]
    for r in range(3):
        for c in range(3):
            total = total + frame[r:r + rows, c:c + cols, :] * w_conv[3 * r + c:3 * r + c + 1, :]
    act = (total * jax.nn.sigmoid(total)).astype(jnp.bfloat16).reshape(tokens, inner)
    act_out[...] = act
    head = dot(act, w_x[...])
    mark = tissue[...].astype(jnp.float32)
    place = lax.broadcasted_iota(jnp.int32, (tokens, 128), 1)
    head_row = jnp.where(place == 112, mark, head[:, :128]).astype(jnp.bfloat16)
    head_col = jnp.where(place == 112, mark, head[:, 128:]).astype(jnp.bfloat16)
    flip = turn(rows, cols)
    head_row = dot(flip, head_row).astype(jnp.bfloat16)
    act_row = dot(flip, act).astype(jnp.bfloat16)
    for part, (msg, n, top, values) in enumerate(
            ((msg_row, nc, head_row, act_row), (msg_col, nr, head_col, act))):
        each = inner // n
        for g in range(n):
            msg[g, :, 0:128] = top
            msg[g, :, 128:128 + each] = values[:, g * each:(g + 1) * each]


def chain_pass(spec, refs, backward, states, outputs):
    chains, steps, width, state = spec
    dt_ref, du_ref, bc_ref, nd_ref, y_ref = refs
    b_at = 32 if backward else 0
    c_at = b_at + state
    col = width if backward else 0
    first = (not backward)

    def one(i, carry):
        held, total = carry
        t = steps - 1 - i if backward else i
        here = pl.ds(pl.multiple_of(t * chains, chains), chains)
        dt = dt_ref[here, col:col + width]
        du = du_ref[here, col:col + width]
        bc = bc_ref[here, :]
        y = None
        fresh = []
        for s in range(state):
            decay = jnp.exp2(nd_ref[s:s + 1, col:col + width] * dt)
            h = decay * held[s] + du * bc[:, b_at + s:b_at + s + 1]
            fresh.append(h)
            if outputs:
                term = h * bc[:, c_at + s:c_at + s + 1]
                y = term if y is None else y + term
        if outputs:
            if first:
                y_ref[here, :] = y
            else:
                y_ref[here, :] = y_ref[here, :] + y
            return tuple(fresh), total
        return tuple(fresh), total + dt

    return lax.fori_loop(0, steps, one, (states, jnp.zeros((chains, width), jnp.float32)), unroll=2)


def scan_kernel(specs, sizes, *refs):
    msgs, weights, biases, nds = refs[0:2], refs[2:4], refs[4:6], refs[6:8]
    ys = refs[8:10]
    scratch = refs[10:]
    greet(sizes)
    work = []
    for p in range(2):
        work.append(scratch[p * 10:(p + 1) * 10])
    for p, (chains, steps, width, each, state) in enumerate(specs):
        dt_s, du_s, bc_s, y_s, end_s, sum_s, slots, send, recv, entry_s = work[p]
        axis, n = sizes[p]
        block = 256

        def prepare(i, unused, p=p, width=width, each=each, dt_s=dt_s, du_s=du_s, bc_s=bc_s):
            here = pl.ds(pl.multiple_of(i * block, block), block)
            head = msgs[p][here, 0:128]
            wide = head.astype(jnp.float32)
            bc_s[here, :] = wide
            x = dot(head, weights[p][...]) + biases[p][...]
            dt = (jnp.maximum(x, 0.0) + jnp.log1p(jnp.exp(-jnp.abs(x)))) * wide[:, 112:113]
            dt_s[here, :] = dt
            act = msgs[p][here, 128:128 + width].astype(jnp.float32)
            if each < width:
                spot = lax.broadcasted_iota(jnp.int32, (block, width), 1)
                act = jnp.where(spot < each, act, 0.0)
            du_s[here, 0:width] = dt[:, 0:width] * act
            du_s[here, width:2 * width] = dt[:, width:2 * width] * act
            return unused

        lax.fori_loop(0, chains * steps // block, prepare, 0)
        me = lax.axis_index(axis)
        for b in range(2):
            col = b * width
            zero = tuple(jnp.zeros((chains, width), jnp.float32) for s in range(state))
            ends, total = chain_pass((chains, steps, width, state),
                                     (dt_s, du_s, bc_s, nds[p], y_s), b == 1, zero, False)
            for s in range(state):
                end_s[b, s] = ends[s]
            sum_s[b] = total
            nd = nds[p][:, col:col + width]
            held = jnp.zeros((state, width), jnp.float32)
            for r in (range(chains - 1, -1, -1) if b else range(chains)):
                held = jnp.exp2(nd * sum_s[b, r:r + 1, :]) * held + end_s[b, :, r, :]
            slots[me, b, 0:state, :] = held
            slots[me, b, state:state + 8, :] = jnp.broadcast_to(
                jnp.sum(total, axis=0, keepdims=True), (8, width))
        for k in range(1, n):
            to = lax.rem(me + k, n)
            pltpu.make_async_remote_copy(
                src_ref=slots.at[me], dst_ref=slots.at[me], send_sem=send.at[k],
                recv_sem=recv.at[k], device_id={axis: to}, device_id_type=MESH).start()
    for p, (chains, steps, width, each, state) in enumerate(specs):
        dt_s, du_s, bc_s, y_s, end_s, sum_s, slots, send, recv, entry_s = work[p]
        axis, n = sizes[p]
        me = lax.axis_index(axis)
        for k in range(1, n):
            to = lax.rem(me + k, n)
            source = lax.rem(me + n - k, n)
            pltpu.make_async_remote_copy(
                src_ref=slots.at[me], dst_ref=slots.at[me], send_sem=send.at[k],
                recv_sem=recv.at[k], device_id={axis: to}, device_id_type=MESH).wait_send()
            pltpu.make_async_remote_copy(
                src_ref=slots.at[source], dst_ref=slots.at[source], send_sem=send.at[k],
                recv_sem=recv.at[k], device_id={axis: to}, device_id_type=MESH).wait_recv()
        for b in range(2):
            col = b * width
            nd = nds[p][:, col:col + width]
            held = jnp.zeros((state, width), jnp.float32)
            for q in (range(n - 1, -1, -1) if b else range(n)):
                ahead = (q > me) if b else (q < me)
                keep = jnp.where(ahead, 1.0, 0.0)
                after = jnp.exp2(nd * slots[q, b, state:state + 1, :]) * held + slots[q, b, 0:state, :]
                held = held + keep * (after - held)
            for r in (range(chains - 1, -1, -1) if b else range(chains)):
                entry_s[:, r, :] = held
                held = jnp.exp2(nd * sum_s[b, r:r + 1, :]) * held + end_s[b, :, r, :]
            start = tuple(entry_s[s] for s in range(state))
            chain_pass((chains, steps, width, state),
                       (dt_s, du_s, bc_s, nds[p], y_s), b == 1, start, True)
        groups = ys[p].shape[0]
        count = chains * steps // groups
        for g in range(groups):
            ys[p][g] = y_s[g * count:(g + 1) * count, 0:each].astype(jnp.bfloat16)


def back_kernel(dims, y_row, y_col, act, gate, skip, gain, w_out, tissue, out, mixed):
    rows, cols, inner, nr, nc = dims
    flip = turn_back(rows, cols)
    each = inner // nc
    for g in range(nc):
        mixed[:, g * each:(g + 1) * each] = dot(flip, y_row[g])
    each = inner // nr
    for g in range(nr):
        here = slice(g * each, (g + 1) * each)
        mixed[:, here] = mixed[:, here] + y_col[g].astype(jnp.float32)
    total = mixed[...] + skip[...] * act[...].astype(jnp.float32)
    centered = total - jnp.mean(total, axis=1, keepdims=True)
    variance = jnp.mean(centered * centered, axis=1, keepdims=True)
    normed = centered * lax.rsqrt(variance + 1e-05) * gain[...]
    gate_wide = gate[...].astype(jnp.float32)
    value = (normed * (gate_wide * jax.nn.sigmoid(gate_wide))).astype(jnp.bfloat16)
    result = dot(value, w_out[...]) * tissue[...].astype(jnp.float32)
    out[...] = result.astype(jnp.bfloat16)


def local_call(kernel, shapes, arrays, scratch, name):
    return pl.pallas_call(
        kernel, out_shape=shapes, in_specs=[VMEM] * len(arrays),
        out_specs=jax.tree.map(lambda unused: VMEM, shapes), scratch_shapes=scratch,
        compiler_params=pltpu.CompilerParams(vmem_limit_bytes=LIMIT), name=name,
    )(*arrays)


def per_device(nr, nc, patches, tissue, in_weight, conv_weight, conv_bias, x_weight, dt_weight,
               dt_bias, decay_rate, skip_gain, norm_gain, out_weight):
    rows, cols, channels = patches.shape
    tokens = rows * cols
    inner = out_weight.shape[0]
    state = decay_rate.shape[2]
    rank = dt_weight.shape[1]
    wide = rank + 2 * state
    r, c = lax.axis_index("row"), lax.axis_index("col")
    bf, f32 = jnp.bfloat16, jnp.float32

    def strip(values):
        return jnp.pad(values, ((0, cols - values.shape[0]), (0, 0)))

    strips = jnp.stack([
        patches[0], patches[-1], strip(patches[:, 0]), strip(patches[:, -1]),
        strip(patches[0, :1]), strip(patches[0, -1:]), strip(patches[-1, :1]), strip(patches[-1, -1:]),
    ])
    got = halo(strips, nr, nc).reshape(8 * cols, channels)
    live = jnp.stack([
        ((r - dr >= 0) & (r - dr < nr) & (c - dc >= 0) & (c - dc < nc)) for dr, dc in AROUND])
    live = jnp.repeat(live.astype(f32), cols)[:, None]

    def heads(first):
        parts = []
        for o in (first, first + 1):
            base = o * wide
            parts.append(x_weight[:, base + rank:base + wide])
        for o in (first, first + 1):
            parts.append(x_weight[:, o * wide:o * wide + rank])
        joined = jnp.concatenate(parts, axis=1)
        return jnp.pad(joined, ((0, 0), (0, 128 - joined.shape[1])))

    w_x = jnp.concatenate([heads(0), heads(2)], axis=1)
    mark = tissue.reshape(tokens, 1)
    dims = (rows, cols, inner, nr, nc)
    each_row, each_col = inner // nc, inner // nr
    shapes = [
        jax.ShapeDtypeStruct((nc, tokens, 128 + lanes(each_row)), bf),
        jax.ShapeDtypeStruct((nr, tokens, 128 + lanes(each_col)), bf),
        jax.ShapeDtypeStruct((tokens, inner), bf),
        jax.ShapeDtypeStruct((tokens, inner), bf),
    ]
    msg_row, msg_col, act, gate = local_call(
        functools.partial(front_kernel, dims), shapes,
        (patches.reshape(tokens, channels), got, live, in_weight, conv_weight.reshape(9, inner),
         conv_bias[None], w_x, mark),
        [pltpu.VMEM((rows + 2, -(-(cols + 2) // 8) * 8, inner), f32)], "front")
    got_row, got_col = swap((("col", nc), ("row", nr)), (msg_row, msg_col), 1)

    def weights(first, place, each):
        width = lanes(each)
        picked = lax.dynamic_slice_in_dim(dt_weight[first:first + 2], place * each, each, 2)
        picked = jnp.pad(picked, ((0, 0), (0, 0), (0, width - each)))
        top = 4 * state
        w = jnp.concatenate([
            jnp.pad(picked[0], ((top, 128 - top - rank), (0, 0))),
            jnp.pad(picked[1], ((top + rank, 128 - top - 2 * rank), (0, 0)))], axis=1)
        bias = lax.dynamic_slice_in_dim(dt_bias[first:first + 2], place * each, each, 1)
        bias = jnp.pad(bias, ((0, 0), (0, width - each))).reshape(1, 2 * width)
        rate = lax.dynamic_slice_in_dim(decay_rate[first:first + 2], place * each, each, 1)
        rate = jnp.pad(jnp.transpose(rate, (2, 0, 1)) * -LOG2E, ((0, 0), (0, 0), (0, width - each)))
        return w, bias, rate.reshape(state, 2 * width)

    w_r, b_r, n_r = weights(0, c, each_row)
    w_c, b_c, n_c = weights(2, r, each_col)
    specs = ((rows, nc * cols, lanes(each_row), each_row, state),
             (cols, nr * rows, lanes(each_col), each_col, state))
    sizes = (("row", nr), ("col", nc))
    scratch = []
    for (chains, steps, width, each, unused), (axis, n) in zip(specs, sizes):
        count = chains * steps
        scratch += [
            pltpu.VMEM((count, 2 * width), f32), pltpu.VMEM((count, 2 * width), f32),
            pltpu.VMEM((count, 128), f32), pltpu.VMEM((count, width), f32),
            pltpu.VMEM((2, state, chains, width), f32), pltpu.VMEM((2, chains, width), f32),
            pltpu.VMEM((n, 2, state + 8, width), f32),
            pltpu.SemaphoreType.DMA((n,)), pltpu.SemaphoreType.DMA((n,)),
            pltpu.VMEM((state, chains, width), f32)]
    y_row, y_col = pl.pallas_call(
        functools.partial(scan_kernel, specs, sizes),
        out_shape=[jax.ShapeDtypeStruct((nc, tokens, each_row), bf),
                   jax.ShapeDtypeStruct((nr, tokens, each_col), bf)],
        in_specs=[VMEM] * 8, out_specs=[VMEM] * 2, scratch_shapes=scratch,
        compiler_params=pltpu.CompilerParams(
            collective_id=2, has_side_effects=True, vmem_limit_bytes=LIMIT),
        name="scan",
    )(got_row.reshape(nc * tokens, -1), got_col.reshape(nr * tokens, -1),
      w_r, w_c, b_r, b_c, n_r, n_c)
    y_row, y_col = swap((("col", nc), ("row", nr)), (y_row, y_col), 3)
    out = local_call(
        functools.partial(back_kernel, dims), jax.ShapeDtypeStruct((tokens, channels), bf),
        (y_row, y_col, act, gate, skip_gain[None], norm_gain[None], out_weight, mark),
        [pltpu.VMEM((tokens, inner), f32)], "back")
    return out.reshape(rows, cols, channels)


def solution(mesh):
    grid = P("row", "col")
    return jax.shard_map(
        functools.partial(per_device, mesh.shape["row"], mesh.shape["col"]), mesh=mesh,
        in_specs=(P("row", "col", None), grid) + (P(),) * 10,
        out_specs=P("row", "col", None), check_vma=False)
```

time: 845 us -> 113 us (0.13)
  the two profiles are of different devices: /device:TPU:24 before, /device:TPU:0 now
where the time goes in v1:
time: 113 us
  Pallas kernels  99.2 us (88%)
  local copies, waits for them, and re-layouts  10.7 us (9%)
  other arithmetic  2.87 us (3%)
    pallas_call x1, Pallas kernels, per_device(): pl.pallas_call(functools.partial(scan_kernel, specs, sizes), out_shape=[j...  60.6 us
    pallas_call x2, Pallas kernels, swap(): pl.pallas_call(functools.partial(swap_kernel, sizes), out_shape=[jax.Shap...  21.3 us
    pallas_call x1, Pallas kernels, halo(): pl.pallas_call(functools.partial(halo_kernel, nr, nc), out_shape=jax.Shap...  10.7 us
    pallas_call x2, Pallas kernels, local_call(): pl.pallas_call(kernel, out_shape=shapes, in_specs=[VMEM] * len(arrays), o...  6.67 us
    unnamed x41, local copies, waits for them, and re-layouts  3.95 us

profile of v1, /device:TPU:0, one launch (start us, length us, event | category | flops | bytes accessed | tf_op | source)
XLA Modules:
  0.0 113.1 jit_solution(564879968834107711)
XLA Ops:
  0.0 0.1 stack.63
  0.1 0.1 broadcast_in_dim.12
  0.2 0.7 broadcast_in_dim_reshape.4.live
  0.9 0.9 fusion.24
  1.8 0.2 copy.30
  2.0 0.2 copy.31
  2.1 0.2 copy.34
  2.3 0.2 copy.35
  2.5 0.8 fusion.25
  3.3 0.2 copy.32
  3.5 0.2 copy.33
  3.6 0.2 copy.36
  3.8 0.2 copy.37
  4.0 0.0 copy-start
  4.0 0.0 copy-start.6
  4.0 0.0 copy-start.4
  4.0 0.6 fusion.12
  4.6 0.0 copy-start.7
  4.6 0.8 pad_maximum_fusion.w_x
  5.5 0.0 copy-done
  5.6 0.0 copy-start.3
  5.6 0.6 copy-done.3
  6.3 10.7 %halo.1 = bf16[8,16,384]{2,1,0:T(8,128)(2,1)} custom-call(bf16[8,16,384]{2,1,0:T(8,128)(2,1)} %copy-done.3), custom_call_target="tpu_custom_call" | custom-call | tf_op jit(solution)/shard_map/halo/pallas_call | solution.py:41
  17.0 0.7 reshape.44.tissue
  17.7 0.6 reshape.35.w_conv
  18.3 0.6 broadcast_in_dim.13.bias
  18.9 3.9 %front.1 = (bf16[4,128,384]{2,1,0:T(8,128)(2,1)}, bf16[8,128,256]{2,1,0:T(8,128)(2,1)}, bf16[128,768]{1,0:T(8,128)(2,1)}, bf16[128,768]{1,0:T(8,128)(2,1)}) custom-call(bf16[128,384]{1,0:T(8,128)(2,1)} %bitcast.63, bf16[128,384]{1,0:T(8,128)(2,1)} %bitcast.61, f32[128,1]{1,0:T(8,128)} %broadcast_in_dim_reshape.4.live, bf16[384,1536]{1,0:T(8,128)(2,1)} %w_in.1, ...), custom_call_target="tpu_custom_call" | custom-call | tf_op jit(solution)/shard_map/front/pallas_call | solution.py:296
  22.8 14.0 %swap1.1 = (bf16[4,128,384]{2,1,0:T(8,128)(2,1)}, bf16[8,128,256]{2,1,0:T(8,128)(2,1)}) custom-call(bf16[4,128,384]{2,1,0:T(8,128)(2,1)} %get-tuple-element.15.refs_0_, bf16[8,128,256]{2,1,0:T(8,128)(2,1)} %get-tuple-element.16.refs_1_), custom_call_target="tpu_custom_call" | custom-call | tf_op jit(solution)/shard_map/swap1/pallas_call | solution.py:87
  36.8 0.1 constant_dynamic-slice_fusion.3
  36.9 0.7 fusion.16.refs_2_
  37.5 0.1 constant_dynamic-slice_fusion.2
  37.6 0.6 fusion.19.refs_3_
  38.3 0.0 copy-done.1
  38.3 0.0 copy-start.9
  38.3 0.1 multiply_bitcast_fusion
  38.5 0.6 copy.41
  39.1 0.1 multiply_bitcast_fusion.1
  39.2 0.6 copy.46
  39.8 0.1 constant_dynamic-slice_fusion.1
  39.9 0.6 copy.40
  40.5 0.1 constant_dynamic-slice_fusion
  40.5 0.6 pad.82
  41.1 60.6 %scan.1 = (bf16[4,128,192]{2,1,0:T(8,128)(2,1)}, bf16[8,128,96]{2,1,0:T(8,128)(2,1)}) custom-call(bf16[512,384]{1,0:T(8,128)(2,1)} %bitcast.62, bf16[1024,256]{1,0:T(8,128)(2,1)} %bitcast.60, bf16[128,512]{1,0:T(8,128)(2,1)} %fusion.16.refs_2_, bf16[128,256]{1,0:T(8,128)(2,1)} %fusion.19.refs_3_, f32[1,512]{1,0:T(1,128)} %bitcast.68, f32[1,256]{1,0:T(1,128)} %bitcast.69, ...), custom_call_target="tpu_custom_call" | custom-call | tf_op jit(solution)/shard_map/scan/pallas_call | solution.py:382
  101.7 7.4 %swap3.1 = (bf16[4,128,192]{2,1,0:T(8,128)(2,1)}, bf16[8,128,96]{2,1,0:T(8,128)(2,1)}) custom-call(bf16[4,128,192]{2,1,0:T(8,128)(2,1)} %get-tuple-element.19.refs_0_, bf16[8,128,96]{2,1,0:T(8,128)(2,1)} %get-tuple-element.20.refs_1_), custom_call_target="tpu_custom_call" | custom-call | tf_op jit(solution)/shard_map/swap3/pallas_call | solution.py:87
  109.1 0.6 broadcast_in_dim.14.skip
  109.7 0.0 copy-done.9
  109.7 0.6 broadcast_in_dim.15.gain
  110.3 2.8 %back.1 = bf16[128,384]{1,0:T(8,128)(2,1)} custom-call(bf16[4,128,192]{2,1,0:T(8,128)(2,1)} %get-tuple-element.21.y_row, bf16[8,128,96]{2,1,0:T(8,128)(2,1)} %get-tuple-element.22.y_col, bf16[128,768]{1,0:T(8,128)(2,1)} %get-tuple-element.23.act, bf16[128,768]{1,0:T(8,128)(2,1)} %get-tuple-element.24.gate, f32[1,768]{1,0:T(1,128)} %broadcast_in_dim.14.skip, ...), custom_call_target="tpu_custom_call" | custom-call | tf_op jit(solution)/shard_map/back/pallas_call | solution.py:296
  (32 shorter events, 0.3 us)
Async XLA Ops:
  4.0 1.5 %copy-start = (bf16[8,16,384]{2,1,0:T(8,128)(2,1)S(1)}, bf16[8,16,384]{2,1,0:T(8,128)(2,1)}, u32[]{:S(2)}) copy-start(bf16[8,16,384]{2,1,0:T(8,128)(2,1)} %param.12) | copy-start | bytes 294916
  4.0 12.9 %copy-start.6 = (s32[8,16]{1,0:T(8,128)S(1)}, s32[8,16]{1,0:T(8,128)}, u32[]{:S(2)}) copy-start(s32[8,16]{1,0:T(8,128)} %param.13) | copy-start | bytes 1540
  4.0 13.7 %copy-start.4 = (f32[3,3,768]{2,1,0:T(4,128)S(1)}, f32[3,3,768]{2,1,0:T(4,128)}, u32[]{:S(2)}) copy-start(f32[3,3,768]{2,1,0:T(4,128)} %param.15) | copy-start | bytes 82948
  4.6 13.7 %copy-start.7 = (f32[768]{0:T(1024)S(1)}, f32[768]{0:T(1024)}, u32[]{:S(2)}) copy-start(f32[768]{0:T(1024)} %param.16) | copy-start | bytes 9220
  5.6 0.6 copy-start.3
  18.9 17.9 %copy-start.2 = (bf16[4,24,768]{2,1,0:T(8,128)(2,1)S(1)}, bf16[4,24,768]{2,1,0:T(8,128)(2,1)}, u32[]{:S(2)}) copy-start(bf16[4,24,768]{2,1,0:T(8,128)(2,1)} %param.18) | copy-start | bytes 442372
  22.8 15.5 %copy-start.1 = (f32[4,768,16]{1,2,0:T(8,128)S(1)}, f32[4,768,16]{1,2,0:T(8,128)}, u32[]{:S(2)}) copy-start(f32[4,768,16]{1,2,0:T(8,128)} %param.20) | copy-start | bytes 589828
  22.8 17.0 %copy-start.5 = (f32[4,768]{1,0:T(4,128)S(1)}, f32[4,768]{1,0:T(4,128)}, u32[]{:S(2)}) copy-start(f32[4,768]{1,0:T(4,128)} %param.19) | copy-start | bytes 36868
  38.3 70.8 %copy-start.8 = (f32[768]{0:T(1024)S(1)}, f32[768]{0:T(1024)}, u32[]{:S(2)}) copy-start(f32[768]{0:T(1024)} %param.21) | copy-start | bytes 9220
  38.3 71.4 %copy-start.9 = (f32[768]{0:T(1024)S(1)}, f32[768]{0:T(1024)}, u32[]{:S(2)}) copy-start(f32[768]{0:T(1024)} %param.22) | copy-start | bytes 9220

commit v2 on v1

v2 whole, which is shorter than its diff:
```python
import functools
import math
import jax
import jax.numpy as jnp
from jax import lax
from jax.experimental import pallas as pl
from jax.experimental.pallas import tpu as pltpu
from jax.sharding import PartitionSpec as P

MESH = pl.DeviceIdType.MESH
VMEM = pl.BlockSpec(memory_space=pltpu.VMEM)
LIMIT = 56 * 1024 * 1024
LOG2E = math.log2(math.e)
AROUND = ((-1, 0), (1, 0), (0, -1), (0, 1), (-1, -1), (-1, 1), (1, -1), (1, 1))


def lanes(width):
    return -(-width // 128) * 128


def greet(peers):
    barrier = pltpu.get_barrier_semaphore()
    for peer in peers:
        pl.semaphore_signal(barrier, inc=1, device_id=peer, device_id_type=MESH)
    pl.semaphore_wait(barrier, len(peers))


def swap(axis, n, src, dst, send, recv, own):
    me = lax.axis_index(axis)
    copies = []
    for k in range(1, n):
        to = lax.rem(me + k, n)
        copies.append(pltpu.make_async_remote_copy(
            src_ref=src.at[to], dst_ref=dst.at[me], send_sem=send.at[k], recv_sem=recv.at[k],
            device_id={axis: to}, device_id_type=MESH))
    copies.append(pltpu.make_async_copy(src.at[me], dst.at[me], own.at[0]))
    for copy in copies:
        copy.start()
    return copies


def finish(copies):
    for copy in copies:
        copy.wait()


def spread(axis, n, slots, send, recv):
    me = lax.axis_index(axis)
    copies = []
    for k in range(1, n):
        copies.append(pltpu.make_async_remote_copy(
            src_ref=slots.at[me], dst_ref=slots.at[me], send_sem=send.at[k], recv_sem=recv.at[k],
            device_id={axis: lax.rem(me + k, n)}, device_id_type=MESH))
    for copy in copies:
        copy.start()
    return copies


def one_hot(hits):
    return hits.astype(jnp.float32).astype(jnp.bfloat16)


def iota(shape, dim):
    return lax.broadcasted_iota(jnp.int32, shape, dim)


def turn(rows, cols):
    count = rows * cols
    out = lax.broadcasted_iota(jnp.int32, (count, count), 0)
    src = lax.broadcasted_iota(jnp.int32, (count, count), 1)
    return (lax.rem(out, rows) * cols + lax.div(out, rows) == src).astype(jnp.float32).astype(jnp.bfloat16)


def turn_back(rows, cols):
    count = rows * cols
    out = lax.broadcasted_iota(jnp.int32, (count, count), 0)
    src = lax.broadcasted_iota(jnp.int32, (count, count), 1)
    return (lax.rem(out, cols) * rows + lax.div(out, cols) == src).astype(jnp.float32).astype(jnp.bfloat16)


def dot(a, b):
    return jnp.dot(a, b, preferred_element_type=jnp.float32)


def rim_picks(rows, cols):
    shape = (8 * cols, rows * cols)
    out, src = iota(shape, 0), iota(shape, 1)
    d, k = lax.div(out, cols), lax.rem(out, cols)
    last = (rows - 1) * cols
    token = jnp.where(d == 0, k, last + k)
    token = jnp.where(d == 2, k * cols, token)
    token = jnp.where(d == 3, k * cols + cols - 1, token)
    token = jnp.where(d == 4, 0, token)
    token = jnp.where(d == 5, cols - 1, token)
    token = jnp.where(d == 6, last, token)
    token = jnp.where(d == 7, rows * cols - 1, token)
    return one_hot(token == src)


def head_picks(columns, rank, state):
    shape = (columns, 256)
    src, out = iota(shape, 0), iota(shape, 1)
    wide = rank + 2 * state
    part, m = lax.div(out, 128), lax.rem(out, 128)
    base = 2 * part * wide
    at = jnp.where(m < 2 * state, base + rank + m, base + wide + rank + m - 2 * state)
    at = jnp.where(m >= 4 * state, base + m - 4 * state, at)
    at = jnp.where(m >= 4 * state + rank, base + wide + m - 4 * state - rank, at)
    at = jnp.where(m >= 4 * state + 2 * rank, -1, at)
    return one_hot(at == src)


def tissue_column(tissue, rows, cols):
    count = rows * cols
    up = one_hot(lax.div(iota((count, rows), 0), cols) == iota((count, rows), 1))
    spread_out = dot(up, tissue[...].astype(jnp.float32).astype(jnp.bfloat16))
    mine = lax.rem(iota((count, cols), 0), cols) == iota((count, cols), 1)
    return jnp.sum(jnp.where(mine, spread_out, 0.0), axis=1, keepdims=True)


def front(dims, rim_copies, patches, rim_in, w_in, w_conv, extras, w_x, tissue,
          msg_row, msg_col, act_out, gate_out, frame):
    rows, cols, inner, nr, nc, rank, state = dims
    tokens = rows * cols
    projected = dot(patches[...], w_in[...])
    gate_out[...] = projected[:, inner:].astype(jnp.bfloat16)
    body = projected[:, :inner].astype(jnp.bfloat16).astype(jnp.float32)
    frame[1:rows + 1, 1:cols + 1, :] = body.reshape(rows, cols, inner)
    finish(rim_copies)
    rim = dot(rim_in[...].reshape(8 * cols, -1), w_in[:, :inner])
    rim = rim.astype(jnp.bfloat16).astype(jnp.float32)
    r, c = lax.axis_index("row"), lax.axis_index("col")
    pieces = []
    for d, (dr, dc) in enumerate(AROUND):
        inside = (r - dr >= 0) & (r - dr < nr) & (c - dc >= 0) & (c - dc < nc)
        pieces.append(rim[d * cols:(d + 1) * cols] * jnp.where(inside, 1.0, 0.0))
    frame[rows + 1, 1:cols + 1, :] = pieces[0]
    frame[0, 1:cols + 1, :] = pieces[1]
    for i in range(rows):
        frame[i + 1, cols + 1:cols + 2, :] = pieces[2][i:i + 1]
        frame[i + 1, 0:1, :] = pieces[3][i:i + 1]
    frame[rows + 1, cols + 1:cols + 2, :] = pieces[4][0:1]
    frame[rows + 1, 0:1, :] = pieces[5][0:1]
    frame[0, cols + 1:cols + 2, :] = pieces[6][0:1]
    frame[0, 0:1, :] = pieces[7][0:1]
    total = jnp.zeros((rows, cols, inner), jnp.float32) + extras[0:1, :]
    for i in range(3):
        for j in range(3):
            total = total + frame[i:i + rows, j:j + cols, :] * w_conv[i, j:j + 1, :]
    act = (total * jax.nn.sigmoid(total)).astype(jnp.bfloat16).reshape(tokens, inner)
    act_out[...] = act
    head = dot(act, w_x[...]).astype(jnp.bfloat16)
    head = dot(head, head_picks(w_x.shape[1], rank, state))
    mark = tissue_column(tissue, rows, cols)
    place = lax.rem(iota((tokens, 256), 1), 128)
    head = jnp.where(place == 4 * state + 2 * rank, mark, head).astype(jnp.bfloat16)
    flip = turn(rows, cols)
    head_row = dot(flip, head[:, :128]).astype(jnp.bfloat16)
    act_row = dot(flip, act).astype(jnp.bfloat16)
    for msg, n, top, values in ((msg_row, nc, head_row, act_row), (msg_col, nr, head[:, 128:], act)):
        each = inner // n
        for g in range(n):
            msg[g, :, 0:128] = top
            msg[g, :, 128:128 + each] = values[:, g * each:(g + 1) * each]


def gather_weights(first, place, each, width, rank, state, dt_weight, dt_bias, decay,
                   wd_s, bias_s, nd_s, ndb_s):
    inner = dt_weight.shape[2]
    shape = (inner, width)
    picks = (iota(shape, 0) == iota(shape, 1) + place * each) & (iota(shape, 1) < each)
    exact = picks.astype(jnp.float32)
    picks = exact.astype(jnp.bfloat16)
    top = 4 * state
    for b in range(2):
        here = slice(b * width, (b + 1) * width)
        w = dot(dt_weight[first + b], picks)
        above = top + b * rank
        w = jnp.concatenate([jnp.zeros((above, width), jnp.float32), w,
                             jnp.zeros((128 - above - rank, width), jnp.float32)], axis=0)
        wd_s[:, here] = w.astype(jnp.bfloat16)
        bias = jnp.broadcast_to(dt_bias[first + b:first + b + 1, :], (8, inner))
        bias_s[:, here] = jnp.dot(bias, exact, precision=lax.Precision.HIGHEST,
                                  preferred_element_type=jnp.float32)
        rate = jnp.dot(decay[first + b], exact, precision=lax.Precision.HIGHEST,
                       preferred_element_type=jnp.float32)
        rate = rate * -LOG2E
        nd_s[:, here] = rate
        for s in range(state):
            ndb_s[s, :, here] = jnp.broadcast_to(rate[s:s + 1], (8, width))


def chain_pass(spec, refs, backward, states, outputs):
    chains, steps, width, state = spec
    dt_ref, du_ref, bc_ref, ndb_ref, y_ref = refs
    b_at = 32 if backward else 0
    c_at = b_at + state
    col = width if backward else 0
    first = (not backward)

    def one(i, carry):
        held, total = carry
        t = steps - 1 - i if backward else i
        here = pl.ds(pl.multiple_of(t * chains, chains), chains)
        dt = dt_ref[here, col:col + width]
        du = du_ref[here, col:col + width]
        bc = bc_ref[here, :]
        y = None
        fresh = []
        for s in range(state):
            rate = ndb_ref[s, :, col:col + width]
            if chains > 8:
                rate = jnp.concatenate([rate] * (chains // 8), axis=0)
            decay = jnp.exp2(rate * dt)
            h = decay * held[s] + du * bc[:, b_at + s:b_at + s + 1]
            fresh.append(h)
            if outputs:
                term = h * bc[:, c_at + s:c_at + s + 1]
                y = term if y is None else y + term
        if outputs:
            if first:
                y_ref[here, :] = y
            else:
                y_ref[here, :] = y_ref[here, :] + y
            return tuple(fresh), total
        return tuple(fresh), total + dt

    return lax.fori_loop(0, steps, one, (states, jnp.zeros((chains, width), jnp.float32)), unroll=4)


def first_pass(spec, n, me, got, wd_s, bias_s, nd_s, ndb_s, dt_s, du_s, bc_s, y_s, end_s, sum_s, slots):
    chains, steps, width, each, rank, state = spec
    senders, block = got.shape[0], got.shape[1]
    mark_at = 4 * state + 2 * rank
    for g in range(senders):
        here = slice(g * block, (g + 1) * block)
        head = got[g, :, 0:128]
        wide = head.astype(jnp.float32)
        bc_s[here, :] = wide
        x = dot(head, wd_s[...]) + bias_s[0:1, :]
        dt = (jnp.maximum(x, 0.0) + jnp.log1p(jnp.exp(-jnp.abs(x)))) * wide[:, mark_at:mark_at + 1]
        dt_s[here, :] = dt
        act = got[g, :, 128:128 + width].astype(jnp.float32)
        if each < width:
            act = jnp.where(iota((block, width), 1) < each, act, 0.0)
        du_s[here, 0:width] = dt[:, 0:width] * act
        du_s[here, width:2 * width] = dt[:, width:2 * width] * act
    for b in range(2):
        col = b * width
        zero = tuple(jnp.zeros((chains, width), jnp.float32) for s in range(state))
        ends, total = chain_pass((chains, steps, width, state),
                                 (dt_s, du_s, bc_s, ndb_s, y_s), b == 1, zero, False)
        for s in range(state):
            end_s[b, s] = ends[s]
        sum_s[b] = total
        nd = nd_s[:, col:col + width]
        held = jnp.zeros((state, width), jnp.float32)
        for r in (range(chains - 1, -1, -1) if b else range(chains)):
            held = jnp.exp2(nd * sum_s[b, r:r + 1, :]) * held + end_s[b, :, r, :]
        slots[me, b, 0:state, :] = held
        slots[me, b, state:state + 8, :] = jnp.broadcast_to(
            jnp.sum(total, axis=0, keepdims=True), (8, width))


def second_pass(spec, n, me, nd_s, ndb_s, dt_s, du_s, bc_s, y_s, end_s, sum_s, slots, entry_s, y_out):
    chains, steps, width, each, rank, state = spec
    for b in range(2):
        col = b * width
        nd = nd_s[:, col:col + width]
        held = jnp.zeros((state, width), jnp.float32)
        for q in (range(n - 1, -1, -1) if b else range(n)):
            ahead = (q > me) if b else (q < me)
            keep = jnp.where(ahead, 1.0, 0.0)
            after = jnp.exp2(nd * slots[q, b, state:state + 1, :]) * held + slots[q, b, 0:state, :]
            held = held + keep * (after - held)
        for r in (range(chains - 1, -1, -1) if b else range(chains)):
            entry_s[:, r, :] = held
            held = jnp.exp2(nd * sum_s[b, r:r + 1, :]) * held + end_s[b, :, r, :]
        start = tuple(entry_s[s] for s in range(state))
        chain_pass((chains, steps, width, state),
                   (dt_s, du_s, bc_s, ndb_s, y_s), b == 1, start, True)
    groups, count = y_out.shape[0], y_out.shape[1]
    for g in range(groups):
        y_out[g] = y_s[g * count:(g + 1) * count, :].astype(jnp.bfloat16)


def kernel(dims, specs, patches, tissue, w_in, w_conv, extras, w_x, dt_weight, dt_bias, decay, w_out,
           out, picked, rim_in, frame, act, gate, mixed, rim_send, rim_recv, *scratch):
    rows, cols, inner, nr, nc, rank, state = dims
    r, c = lax.axis_index("row"), lax.axis_index("col")
    near = [(lax.rem(r + dr + nr, nr), lax.rem(c + dc + nc, nc)) for dr, dc in AROUND]
    peers = near[4:]
    peers += [(lax.rem(r + k, nr), c) for k in range(1, nr)]
    peers += [(r, lax.rem(c + k, nc)) for k in range(1, nc)]
    picked[...] = dot(rim_picks(rows, cols), patches[...]).astype(jnp.bfloat16).reshape(picked.shape)
    greet(peers)
    rim_copies = []
    for d, peer in enumerate(near):
        rim_copies.append(pltpu.make_async_remote_copy(
            src_ref=picked.at[d], dst_ref=rim_in.at[d], send_sem=rim_send.at[d],
            recv_sem=rim_recv.at[d], device_id=peer, device_id_type=MESH))
        rim_copies[-1].start()
    half = len(scratch) // 2
    row, col = scratch[:half], scratch[half:]
    parts = ((row, "col", nc, c, "row", nr, r, specs[0], 0), (col, "row", nr, r, "col", nc, c, specs[1], 2))
    for work, axis, n, me, chain, m, place, spec, first in parts:
        gather_weights(first, me, spec[3], spec[2], rank, state, dt_weight, dt_bias, decay, *work[13:17])
    front(dims, rim_copies, patches, rim_in, w_in, w_conv, extras, w_x, tissue,
          row[0], col[0], act, gate, frame)
    away = [swap(axis, n, work[0], work[1], *work[4:7]) for work, axis, n, *unused in parts]
    sums = []
    for p, (work, axis, n, me, chain, m, place, spec, first) in enumerate(parts):
        finish(away[p])
        first_pass(spec, m, place, work[1], *work[13:23], work[23])
        sums.append(spread(chain, m, work[23], work[10], work[11]))
    home = []
    for p, (work, axis, n, me, chain, m, place, spec, first) in enumerate(parts):
        finish(sums[p])
        second_pass(spec, m, place, *work[15:24], work[12], work[2])
        home.append(swap(axis, n, work[2], work[3], *work[7:10]))
    finish(home[0])
    flip = turn_back(rows, cols)
    each = inner // nc
    for g in range(nc):
        mixed[:, g * each:(g + 1) * each] = dot(flip, row[3][g])[:, :each]
    finish(home[1])
    each = inner // nr
    for g in range(nr):
        here = slice(g * each, (g + 1) * each)
        mixed[:, here] = mixed[:, here] + col[3][g].astype(jnp.float32)[:, :each]
    total = mixed[...] + extras[1:2, :] * act[...].astype(jnp.float32)
    centered = total - jnp.mean(total, axis=1, keepdims=True)
    variance = jnp.mean(centered * centered, axis=1, keepdims=True)
    normed = centered * lax.rsqrt(variance + 1e-05) * extras[2:3, :]
    gate_wide = gate[...].astype(jnp.float32)
    value = (normed * (gate_wide * jax.nn.sigmoid(gate_wide))).astype(jnp.bfloat16)
    result = dot(value, w_out[...]) * tissue_column(tissue, rows, cols)
    out[...] = result.astype(jnp.bfloat16)


def per_device(nr, nc, patches, tissue, in_weight, conv_weight, conv_bias, x_weight, dt_weight,
               dt_bias, decay_rate, skip_gain, norm_gain, out_weight):
    rows, cols, channels = patches.shape
    tokens = rows * cols
    inner = out_weight.shape[0]
    state = decay_rate.shape[2]
    rank = dt_weight.shape[1]
    bf, f32 = jnp.bfloat16, jnp.float32
    dma = pltpu.SemaphoreType.DMA
    dims = (rows, cols, inner, nr, nc, rank, state)
    specs, scratch = [], [
        pltpu.VMEM((8, cols, channels), bf), pltpu.VMEM((8, cols, channels), bf),
        pltpu.VMEM((rows + 2, -(-(cols + 2) // 8) * 8, inner), f32),
        pltpu.VMEM((tokens, inner), bf), pltpu.VMEM((tokens, inner), bf),
        pltpu.VMEM((tokens, inner), f32), dma((8,)), dma((8,))]
    for chains, n, m, length in ((rows, nc, nr, cols), (cols, nr, nc, rows)):
        each = inner // n
        width = lanes(each)
        steps = n * length
        specs.append((chains, steps, width, each, rank, state))
        count = chains * steps
        scratch += [
            pltpu.VMEM((n, tokens, 128 + width), bf), pltpu.VMEM((n, tokens, 128 + width), bf),
            pltpu.VMEM((n, tokens, width), bf), pltpu.VMEM((n, tokens, width), bf),
            dma((n,)), dma((n,)), dma((1,)), dma((n,)), dma((n,)), dma((1,)), dma((m,)), dma((m,)),
            pltpu.VMEM((state, chains, width), f32),
            pltpu.VMEM((128, 2 * width), bf), pltpu.VMEM((8, 2 * width), f32),
            pltpu.VMEM((state, 2 * width), f32), pltpu.VMEM((state, 8, 2 * width), f32),
            pltpu.VMEM((count, 2 * width), f32), pltpu.VMEM((count, 2 * width), f32),
            pltpu.VMEM((count, 128), f32), pltpu.VMEM((count, width), f32),
            pltpu.VMEM((2, state, chains, width), f32), pltpu.VMEM((2, chains, width), f32),
            pltpu.VMEM((m, 2, state + 8, width), f32)]
    extras = jnp.stack([conv_bias, skip_gain, norm_gain])
    out = pl.pallas_call(
        functools.partial(kernel, dims, specs),
        out_shape=jax.ShapeDtypeStruct((tokens, channels), bf),
        in_specs=[VMEM] * 10, out_specs=VMEM, scratch_shapes=scratch,
        compiler_params=pltpu.CompilerParams(
            collective_id=0, has_side_effects=True, vmem_limit_bytes=LIMIT),
        name="block",
    )(patches.reshape(tokens, channels), tissue, in_weight, conv_weight, extras, x_weight,
      dt_weight, dt_bias, jnp.transpose(decay_rate, (0, 2, 1)), out_weight)
    return out.reshape(rows, cols, channels)


def solution(mesh):
    grid = P("row", "col")
    return jax.shard_map(
        functools.partial(per_device, mesh.shape["row"], mesh.shape["col"]), mesh=mesh,
        in_specs=(P("row", "col", None), grid) + (P(),) * 10,
        out_specs=P("row", "col", None), check_vma=False)
```

time: 113 us -> 76.4 us (0.68)
  Pallas kernels: 99.2 us -> 69.9 us
  local copies, waits for them, and re-layouts: 10.7 us -> 5.5 us
  other arithmetic: 2.87 us -> 0.61 us
    pallas_call x6 -> x1, Pallas kernels: 99.2 us -> 69.9 us  [per_device(): pl.pallas_call(functools.partial(kernel, dims, specs), out_shape=jax.Shap...]
    concatenate x4 -> x0, other arithmetic: 2.71 us -> none  [the longest x2 1.3 us: weights(): jnp.concatenate([jnp.pad(picked[0], ((top, 128 - top - rank), (0, 0))), j...]
    broadcast_in_dim x4 -> x0, local copies, waits for them, and re-layouts: 1.83 us -> none  [the longest x1 0.59 us: per_device(): conv_bias[None]]
    slice x6 -> x0, local copies, waits for them, and re-layouts: 1.78 us -> none  [the longest x1 0.88 us: heads(): parts.append(x_weight[:, base + rank:base + wide])]
    reshape x2 -> x0, local copies, waits for them, and re-layouts: 1.35 us -> none  [the longest x1 0.71 us: per_device(): mark = tissue.reshape(tokens, 1)]
    another operation x3, local copies, waits for them, and re-layouts: 0.83 us -> 2.07 us  [per_device(): extras = jnp.stack([conv_bias, skip_gain, norm_gain])]
    unnamed x41 -> x2, local copies, waits for them, and re-layouts: 3.95 us -> 3.43 us
where the time goes in v2:
time: 76.4 us; the launch traced here: 76 us
  Pallas kernels  69.9 us (91%)
  local copies, waits for them, and re-layouts  5.5 us (7%)
    pallas_call x1, Pallas kernels, per_device(): pl.pallas_call(functools.partial(kernel, dims, specs), out_shape=jax.Shap...  69.9 us
    unnamed x2, local copies, waits for them, and re-layouts  3.43 us
    another operation x3, local copies, waits for them, and re-layouts, per_device(): extras = jnp.stack([conv_bias, skip_gain, norm_gain])  2.07 us

profile of v2, /device:TPU:0, one launch (start us, length us, event | category | flops | bytes accessed | tf_op | source)
XLA Modules:
  0.0 76.0 jit_solution(10524197501976234593)
XLA Ops:
  0.0 0.7 stack.12
  0.7 0.7 stack.13
  1.4 0.7 stack.14
  2.1 0.6 pad_maximum_fusion.extras
  2.7 1.9 %copy.13.w_x = bf16[768,224]{1,0:T(8,128)(2,1)} copy(bf16[768,224]{0,1:T(8,128)(2,1)} %param.17) | data formatting | bytes 688128 | tf_op args[5]
  4.6 69.9 %block.1 = bf16[128,384]{1,0:T(8,128)(2,1)} custom-call(bf16[128,384]{1,0:T(8,128)(2,1)} %bitcast.5, s32[8,16]{1,0:T(8,128)} %tissue.1, bf16[384,1536]{1,0:T(8,128)(2,1)} %w_in.1, f32[3,3,768]{2,1,0:T(4,128)} %w_conv.1, f32[3,768]{1,0:T(4,128)} %pad_maximum_fusion.extras, bf16[768,224]{1,0:T(8,128)(2,1)} %copy.13.w_x, bf16[4,24,768]{2,1,0:T(8,128)(2,1)} %dt_weight.1, ...), custom_call_target="tpu_custom_call" | custom-call | tf_op jit(solution)/shard_map/block/pallas_call | solution.py:374
  74.5 1.5 %copy.15 = bf16[8,16,384]{2,1,0:T(8,128)(2,1)} copy(bf16[8,16,384]{2,1,0:T(8,128)(2,1)} %bitcast.3) | data formatting | bytes 196608

commit v3 on v2

--- a/solution.py
+++ b/solution.py
@@ -9,6 +9,7 @@
 
 MESH = pl.DeviceIdType.MESH
 VMEM = pl.BlockSpec(memory_space=pltpu.VMEM)
+GROUP = 4
 LIMIT = 56 * 1024 * 1024
 LOG2E = math.log2(math.e)
 AROUND = ((-1, 0), (1, 0), (0, -1), (0, 1), (-1, -1), (-1, 1), (1, -1), (1, 1))
@@ -118,7 +119,7 @@
     return jnp.sum(jnp.where(mine, spread_out, 0.0), axis=1, keepdims=True)
 
 
-def front(dims, rim_copies, patches, rim_in, w_in, w_conv, extras, w_x, tissue,
+def front(dims, rim_copies, patches, rim_in, w_in, w_conv, bias, w_x, tissue,
           msg_row, msg_col, act_out, gate_out, frame):
     rows, cols, inner, nr, nc, rank, state = dims
     tokens = rows * cols
@@ -143,14 +144,15 @@
     frame[rows + 1, 0:1, :] = pieces[5][0:1]
     frame[0, cols + 1:cols + 2, :] = pieces[6][0:1]
     frame[0, 0:1, :] = pieces[7][0:1]
-    total = jnp.zeros((rows, cols, inner), jnp.float32) + extras[0:1, :]
+    total = jnp.zeros((rows, cols, inner), jnp.float32) + bias[...].reshape(1, inner)
     for i in range(3):
         for j in range(3):
             total = total + frame[i:i + rows, j:j + cols, :] * w_conv[i, j:j + 1, :]
     act = (total * jax.nn.sigmoid(total)).astype(jnp.bfloat16).reshape(tokens, inner)
     act_out[...] = act
-    head = dot(act, w_x[...]).astype(jnp.bfloat16)
-    head = dot(head, head_picks(w_x.shape[1], rank, state))
+    head = lax.dot_general(act, w_x[...], (((1,), (1,)), ((), ())),
+                           preferred_element_type=jnp.float32).astype(jnp.bfloat16)
+    head = dot(head, head_picks(w_x.shape[0], rank, state))
     mark = tissue_column(tissue, rows, cols)
     place = lax.rem(iota((tokens, 256), 1), 128)
     head = jnp.where(place == 4 * state + 2 * rank, mark, head).astype(jnp.bfloat16)
@@ -164,13 +166,19 @@
             msg[g, :, 128:128 + each] = values[:, g * each:(g + 1) * each]
 
 
+def pick_exact(values, picks):
+    high = values.astype(jnp.bfloat16)
+    rest = values - high.astype(jnp.float32)
+    middle = rest.astype(jnp.bfloat16)
+    low = (rest - middle.astype(jnp.float32)).astype(jnp.bfloat16)
+    return dot(high, picks) + dot(middle, picks) + dot(low, picks)
+
+
 def gather_weights(first, place, each, width, rank, state, dt_weight, dt_bias, decay,
                    wd_s, bias_s, nd_s, ndb_s):
     inner = dt_weight.shape[2]
     shape = (inner, width)
-    picks = (iota(shape, 0) == iota(shape, 1) + place * each) & (iota(shape, 1) < each)
-    exact = picks.astype(jnp.float32)
-    picks = exact.astype(jnp.bfloat16)
+    picks = one_hot((iota(shape, 0) == iota(shape, 1) + place * each) & (iota(shape, 1) < each))
     top = 4 * state
     for b in range(2):
         here = slice(b * width, (b + 1) * width)
@@ -180,55 +188,64 @@
                              jnp.zeros((128 - above - rank, width), jnp.float32)], axis=0)
         wd_s[:, here] = w.astype(jnp.bfloat16)
         bias = jnp.broadcast_to(dt_bias[first + b:first + b + 1, :], (8, inner))
-        bias_s[:, here] = jnp.dot(bias, exact, precision=lax.Precision.HIGHEST,
-                                  preferred_element_type=jnp.float32)
-        rate = jnp.dot(decay[first + b], exact, precision=lax.Precision.HIGHEST,
-                       preferred_element_type=jnp.float32)
-        rate = rate * -LOG2E
+        bias_s[:, here] = pick_exact(bias, picks)
+        rate = pick_exact(decay[first + b], picks) * -LOG2E
         nd_s[:, here] = rate
         for s in range(state):
             ndb_s[s, :, here] = jnp.broadcast_to(rate[s:s + 1], (8, width))
 
 
+def full(rate, chains):
+    return rate if chains == 8 else jnp.concatenate([rate] * (chains // 8), axis=0)
+
+
 def chain_pass(spec, refs, backward, states, outputs):
     chains, steps, width, state = spec
     dt_ref, du_ref, bc_ref, ndb_ref, y_ref = refs
-    b_at = 32 if backward else 0
+    b_at = 2 * state if backward else 0
     c_at = b_at + state
     col = width if backward else 0
-    first = (not backward)
-
-    def one(i, carry):
-        held, total = carry
-        t = steps - 1 - i if backward else i
-        here = pl.ds(pl.multiple_of(t * chains, chains), chains)
-        dt = dt_ref[here, col:col + width]
-        du = du_ref[here, col:col + width]
-        bc = bc_ref[here, :]
-        y = None
-        fresh = []
-        for s in range(state):
-            rate = ndb_ref[s, :, col:col + width]
-            if chains > 8:
-                rate = jnp.concatenate([rate] * (chains // 8), axis=0)
-            decay = jnp.exp2(rate * dt)
-            h = decay * held[s] + du * bc[:, b_at + s:b_at + s + 1]
-            fresh.append(h)
+    ends = []
+    summed = None
+    for low in range(0, state, GROUP):
+        group = range(low, low + GROUP)
+        rates = [full(ndb_ref[s, :, col:col + width], chains) for s in group]
+        write = low == 0 and not backward
+        count = low == 0 and not outputs
+
+        def one(i, carry, group=group, rates=rates, write=write, count=count):
+            held, total = carry
+            t = steps - 1 - i if backward else i
+            here = pl.ds(pl.multiple_of(t * chains, chains), chains)
+            dt = dt_ref[here, col:col + width]
+            du = du_ref[here, col:col + width]
+            bc = bc_ref[here, :]
+            fresh, terms = [], []
+            for s, rate, before in zip(group, rates, held):
+                h = jnp.exp2(rate * dt) * before + du * bc[:, b_at + s:b_at + s + 1]
+                fresh.append(h)
+                if outputs:
+                    terms.append(h * bc[:, c_at + s:c_at + s + 1])
             if outputs:
-                term = h * bc[:, c_at + s:c_at + s + 1]
-                y = term if y is None else y + term
-        if outputs:
-            if first:
-                y_ref[here, :] = y
-            else:
-                y_ref[here, :] = y_ref[here, :] + y
-            return tuple(fresh), total
-        return tuple(fresh), total + dt
-
-    return lax.fori_loop(0, steps, one, (states, jnp.zeros((chains, width), jnp.float32)), unroll=4)
-
-
-def first_pass(spec, n, me, got, wd_s, bias_s, nd_s, ndb_s, dt_s, du_s, bc_s, y_s, end_s, sum_s, slots):
+                y = (terms[0] + terms[1]) + (terms[2] + terms[3])
+                y_ref[here, :] = y if write else y_ref[here, :] + y
+            return tuple(fresh), total + dt if count else total
+
+        start = jnp.zeros((chains, width), jnp.float32) if count else 0
+        held, total = lax.fori_loop(0, steps, one, (tuple(states[low:low + GROUP]), start), unroll=8)
+        ends += held
+        summed = total if count else summed
+    return ends, summed
+
+
+def shifted(values, by, backward):
+    edge = jnp.zeros((by, values.shape[1]), jnp.float32)
+    if backward:
+        return jnp.concatenate([values[by:], edge], axis=0)
+    return jnp.concatenate([edge, values[:-by]], axis=0)
+
+
+def first_pass(spec, n, me, got, wd_s, bias_s, nd_s, ndb_s, dt_s, du_s, bc_s, y_s, entry_s, sum_s, slots):
     chains, steps, width, each, rank, state = spec
     senders, block = got.shape[0], got.shape[1]
     mark_at = 4 * state + 2 * rank
@@ -247,22 +264,25 @@
         du_s[here, width:2 * width] = dt[:, width:2 * width] * act
     for b in range(2):
         col = b * width
-        zero = tuple(jnp.zeros((chains, width), jnp.float32) for s in range(state))
+        zero = [jnp.zeros((chains, width), jnp.float32)] * state
         ends, total = chain_pass((chains, steps, width, state),
                                  (dt_s, du_s, bc_s, ndb_s, y_s), b == 1, zero, False)
+        rates = [full(ndb_s[s, :, col:col + width], chains) for s in range(state)]
+        by = 1
+        while by < chains:
+            ends = [jnp.exp2(rate * total) * shifted(end, by, b == 1) + end
+                    for rate, end in zip(rates, ends)]
+            total = total + shifted(total, by, b == 1)
+            by *= 2
+        last = 0 if b else chains - 1
         for s in range(state):
-            end_s[b, s] = ends[s]
-        sum_s[b] = total
-        nd = nd_s[:, col:col + width]
-        held = jnp.zeros((state, width), jnp.float32)
-        for r in (range(chains - 1, -1, -1) if b else range(chains)):
-            held = jnp.exp2(nd * sum_s[b, r:r + 1, :]) * held + end_s[b, :, r, :]
-        slots[me, b, 0:state, :] = held
-        slots[me, b, state:state + 8, :] = jnp.broadcast_to(
-            jnp.sum(total, axis=0, keepdims=True), (8, width))
-
-
-def second_pass(spec, n, me, nd_s, ndb_s, dt_s, du_s, bc_s, y_s, end_s, sum_s, slots, entry_s, y_out):
+            slots[me, b, s:s + 1, :] = ends[s][last:last + 1]
+            entry_s[b, s] = shifted(ends[s], 1, b == 1)
+        slots[me, b, state:state + 8, :] = jnp.broadcast_to(total[last:last + 1], (8, width))
+        sum_s[b] = shifted(total, 1, b == 1)
+
+
+def second_pass(spec, n, me, nd_s, ndb_s, dt_s, du_s, bc_s, y_s, entry_s, sum_s, slots, y_out):
     chains, steps, width, each, rank, state = spec
     for b in range(2):
         col = b * width
@@ -273,10 +293,9 @@
             keep = jnp.where(ahead, 1.0, 0.0)
             after = jnp.exp2(nd * slots[q, b, state:state + 1, :]) * held + slots[q, b, 0:state, :]
             held = held + keep * (after - held)
-        for r in (range(chains - 1, -1, -1) if b else range(chains)):
-            entry_s[:, r, :] = held
-            held = jnp.exp2(nd * sum_s[b, r:r + 1, :]) * held + end_s[b, :, r, :]
-        start = tuple(entry_s[s] for s in range(state))
+        start = [
+            jnp.exp2(full(ndb_s[s, :, col:col + width], chains) * sum_s[b]) * held[s:s + 1]
+            + entry_s[b, s] for s in range(state)]
         chain_pass((chains, steps, width, state),
                    (dt_s, du_s, bc_s, ndb_s, y_s), b == 1, start, True)
     groups, count = y_out.shape[0], y_out.shape[1]
@@ -284,8 +303,8 @@
         y_out[g] = y_s[g * count:(g + 1) * count, :].astype(jnp.bfloat16)
 
 
-def kernel(dims, specs, patches, tissue, w_in, w_conv, extras, w_x, dt_weight, dt_bias, decay, w_out,
-           out, picked, rim_in, frame, act, gate, mixed, rim_send, rim_recv, *scratch):
+def kernel(dims, specs, patches, tissue, w_in, w_conv, bias, skip, gain, w_x, dt_weight, dt_bias, decay,
+           w_out, out, picked, rim_in, frame, act, gate, mixed, rim_send, rim_recv, *scratch):
     rows, cols, inner, nr, nc, rank, state = dims
     r, c = lax.axis_index("row"), lax.axis_index("col")
     near = [(lax.rem(r + dr + nr, nr), lax.rem(c + dc + nc, nc)) for dr, dc in AROUND]
@@ -303,11 +322,11 @@
     half = len(scratch) // 2
     row, col = scratch[:half], scratch[half:]
     parts = ((row, "col", nc, c, "row", nr, r, specs[0], 0), (col, "row", nr, r, "col", nc, c, specs[1], 2))
+    front(dims, rim_copies, patches, rim_in, w_in, w_conv, bias, w_x, tissue,
+          row[0], col[0], act, gate, frame)
+    away = [swap(axis, n, work[0], work[1], *work[4:7]) for work, axis, n, *unused in parts]
     for work, axis, n, me, chain, m, place, spec, first in parts:
         gather_weights(first, me, spec[3], spec[2], rank, state, dt_weight, dt_bias, decay, *work[13:17])
-    front(dims, rim_copies, patches, rim_in, w_in, w_conv, extras, w_x, tissue,
-          row[0], col[0], act, gate, frame)
-    away = [swap(axis, n, work[0], work[1], *work[4:7]) for work, axis, n, *unused in parts]
     sums = []
     for p, (work, axis, n, me, chain, m, place, spec, first) in enumerate(parts):
         finish(away[p])
@@ -316,7 +335,7 @@
     home = []
     for p, (work, axis, n, me, chain, m, place, spec, first) in enumerate(parts):
         finish(sums[p])
-        second_pass(spec, m, place, *work[15:24], work[12], work[2])
+        second_pass(spec, m, place, *work[15:24], work[2])
         home.append(swap(axis, n, work[2], work[3], *work[7:10]))
     finish(home[0])
     flip = turn_back(rows, cols)
@@ -328,14 +347,14 @@
     for g in range(nr):
         here = slice(g * each, (g + 1) * each)
         mixed[:, here] = mixed[:, here] + col[3][g].astype(jnp.float32)[:, :each]
-    total = mixed[...] + extras[1:2, :] * act[...].astype(jnp.float32)
+    total = mixed[...] + skip[...].reshape(1, inner) * act[...].astype(jnp.float32)
     centered = total - jnp.mean(total, axis=1, keepdims=True)
     variance = jnp.mean(centered * centered, axis=1, keepdims=True)
-    normed = centered * lax.rsqrt(variance + 1e-05) * extras[2:3, :]
+    normed = centered * lax.rsqrt(variance + 1e-05) * gain[...].reshape(1, inner)
     gate_wide = gate[...].astype(jnp.float32)
     value = (normed * (gate_wide * jax.nn.sigmoid(gate_wide))).astype(jnp.bfloat16)
     result = dot(value, w_out[...]) * tissue_column(tissue, rows, cols)
-    out[...] = result.astype(jnp.bfloat16)
+    out[...] = result
 
 
 def per_device(nr, nc, patches, tissue, in_weight, conv_weight, conv_bias, x_weight, dt_weight,
@@ -363,24 +382,23 @@
             pltpu.VMEM((n, tokens, 128 + width), bf), pltpu.VMEM((n, tokens, 128 + width), bf),
             pltpu.VMEM((n, tokens, width), bf), pltpu.VMEM((n, tokens, width), bf),
             dma((n,)), dma((n,)), dma((1,)), dma((n,)), dma((n,)), dma((1,)), dma((m,)), dma((m,)),
-            pltpu.VMEM((state, chains, width), f32),
+            dma((1,)),
             pltpu.VMEM((128, 2 * width), bf), pltpu.VMEM((8, 2 * width), f32),
             pltpu.VMEM((state, 2 * width), f32), pltpu.VMEM((state, 8, 2 * width), f32),
             pltpu.VMEM((count, 2 * width), f32), pltpu.VMEM((count, 2 * width), f32),
             pltpu.VMEM((count, 128), f32), pltpu.VMEM((count, width), f32),
             pltpu.VMEM((2, state, chains, width), f32), pltpu.VMEM((2, chains, width), f32),
             pltpu.VMEM((m, 2, state + 8, width), f32)]
-    extras = jnp.stack([conv_bias, skip_gain, norm_gain])
     out = pl.pallas_call(
         functools.partial(kernel, dims, specs),
-        out_shape=jax.ShapeDtypeStruct((tokens, channels), bf),
-        in_specs=[VMEM] * 10, out_specs=VMEM, scratch_shapes=scratch,
+        out_shape=jax.ShapeDtypeStruct((tokens, channels), f32),
+        in_specs=[VMEM] * 12, out_specs=VMEM, scratch_shapes=scratch,
         compiler_params=pltpu.CompilerParams(
             collective_id=0, has_side_effects=True, vmem_limit_bytes=LIMIT),
         name="block",
-    )(patches.reshape(tokens, channels), tissue, in_weight, conv_weight, extras, x_weight,
+    )(patches.reshape(tokens, channels), tissue, in_weight, conv_weight, conv_bias, skip_gain, norm_gain, x_weight.T,
       dt_weight, dt_bias, jnp.transpose(decay_rate, (0, 2, 1)), out_weight)
-    return out.reshape(rows, cols, channels)
+    return out.astype(bf).reshape(rows, cols, channels)
 
 
 def solution(mesh):

time: 76.4 us -> 79.1 us (1.035)
  Pallas kernels: 69.9 us -> 77.3 us
  local copies, waits for them, and re-layouts: 5.5 us -> 0 us
  other arithmetic: 0.61 us -> 1.58 us
    pallas_call x1, Pallas kernels: 69.9 us -> 77.3 us  [per_device(): pl.pallas_call(functools.partial(kernel, dims, specs), out_shape=jax.Shap...]
    unnamed x2 -> x0, local copies, waits for them, and re-layouts: 3.43 us -> none
    another operation x3 -> x0, local copies, waits for them, and re-layouts: 2.07 us -> none  [per_device(): extras = jnp.stack([conv_bias, skip_gain, norm_gain])]
    convert_element_type x0 -> x1, other arithmetic: none -> 1.58 us  [per_device(): return out.astype(bf).reshape(rows, cols, channels)]
where the time goes in v3:
time: 79.1 us; the launch traced here: 78.8 us
  Pallas kernels  77.3 us (98%)
  other arithmetic  1.58 us (2%)
    pallas_call x1, Pallas kernels, per_device(): pl.pallas_call(functools.partial(kernel, dims, specs), out_shape=jax.Shap...  77.3 us

profile of v3, /device:TPU:0, one launch (start us, length us, event | category | flops | bytes accessed | tf_op | source)
XLA Modules:
  0.0 78.8 jit_solution(13584822839779222280)
XLA Ops:
  0.0 77.3 %block.1 = f32[128,384]{1,0:T(8,128)} custom-call(bf16[128,384]{1,0:T(8,128)(2,1)} %bitcast.6, s32[8,16]{1,0:T(8,128)} %tissue.1, bf16[384,1536]{1,0:T(8,128)(2,1)} %w_in.1, f32[3,3,768]{2,1,0:T(4,128)} %w_conv.1, f32[768]{0:T(1024)} %bias.1, f32[768]{0:T(1024)} %skip.1, f32[768]{0:T(1024)} %gain.1, bf16[224,768]{1,0:T(8,128)(2,1)} %bitcast.4, ...), custom_call_target="tpu_custom_call" | custom-call | tf_op jit(solution)/shard_map/block/pallas_call | solution.py:392
  77.3 1.6 %convert_element_type.3 = bf16[128,384]{1,0:T(8,128)(2,1)} convert(f32[128,384]{1,0:T(8,128)} %block.1) | non-fusion elementwise | flops 49152 | bytes 294912 | tf_op jit(solution)/shard_map/convert_element_type | solution.py:401

commit v4 on v3

--- a/solution.py
+++ b/solution.py
@@ -9,7 +9,6 @@
 
 MESH = pl.DeviceIdType.MESH
 VMEM = pl.BlockSpec(memory_space=pltpu.VMEM)
-GROUP = 4
 LIMIT = 56 * 1024 * 1024
 LOG2E = math.log2(math.e)
 AROUND = ((-1, 0), (1, 0), (0, -1), (0, 1), (-1, -1), (-1, 1), (1, -1), (1, 1))
@@ -205,37 +204,29 @@
     b_at = 2 * state if backward else 0
     c_at = b_at + state
     col = width if backward else 0
-    ends = []
-    summed = None
-    for low in range(0, state, GROUP):
-        group = range(low, low + GROUP)
-        rates = [full(ndb_ref[s, :, col:col + width], chains) for s in group]
-        write = low == 0 and not backward
-        count = low == 0 and not outputs
-
-        def one(i, carry, group=group, rates=rates, write=write, count=count):
-            held, total = carry
-            t = steps - 1 - i if backward else i
-            here = pl.ds(pl.multiple_of(t * chains, chains), chains)
-            dt = dt_ref[here, col:col + width]
-            du = du_ref[here, col:col + width]
-            bc = bc_ref[here, :]
-            fresh, terms = [], []
-            for s, rate, before in zip(group, rates, held):
-                h = jnp.exp2(rate * dt) * before + du * bc[:, b_at + s:b_at + s + 1]
-                fresh.append(h)
-                if outputs:
-                    terms.append(h * bc[:, c_at + s:c_at + s + 1])
+
+    def one(i, carry):
+        held, total = carry
+        t = steps - 1 - i if backward else i
+        here = pl.ds(pl.multiple_of(t * chains, chains), chains)
+        dt = dt_ref[here, col:col + width]
+        du = du_ref[here, col:col + width]
+        bc = bc_ref[here, :]
+        y = y_ref[here, :] if outputs and backward else None
+        fresh = []
+        for s in range(state):
+            rate = full(ndb_ref[s, :, col:col + width], chains)
+            h = jnp.exp2(rate * dt) * held[s] + du * bc[:, b_at + s:b_at + s + 1]
+            fresh.append(h)
             if outputs:
-                y = (terms[0] + terms[1]) + (terms[2] + terms[3])
-                y_ref[here, :] = y if write else y_ref[here, :] + y
-            return tuple(fresh), total + dt if count else total
-
-        start = jnp.zeros((chains, width), jnp.float32) if count else 0
-        held, total = lax.fori_loop(0, steps, one, (tuple(states[low:low + GROUP]), start), unroll=8)
-        ends += held
-        summed = total if count else summed
-    return ends, summed
+                term = h * bc[:, c_at + s:c_at + s + 1]
+                y = term if y is None else y + term
+        if outputs:
+            y_ref[here, :] = y
+        return tuple(fresh), total if outputs else total + dt
+
+    start = 0 if outputs else jnp.zeros((chains, width), jnp.float32)
+    return lax.fori_loop(0, steps, one, (tuple(states), start), unroll=8)
 
 
 def shifted(values, by, backward):

time: 79.1 us -> 68.7 us (0.87)
  Pallas kernels: 77.3 us -> 66.9 us
    pallas_call x1, Pallas kernels: 77.3 us -> 66.9 us  [per_device(): pl.pallas_call(functools.partial(kernel, dims, specs), out_shape=jax.Shap...]
where the time goes in v4:
time: 68.7 us; the launch traced here: 68.5 us
  Pallas kernels  66.9 us (97%)
  other arithmetic  1.58 us (2%)
    pallas_call x1, Pallas kernels, per_device(): pl.pallas_call(functools.partial(kernel, dims, specs), out_shape=jax.Shap...  66.9 us
    convert_element_type x1, other arithmetic, per_device(): return out.astype(bf).reshape(rows, cols, channels)  1.58 us

profile of v4, /device:TPU:0, one launch (start us, length us, event | category | flops | bytes accessed | tf_op | source)
XLA Modules:
  0.0 68.5 jit_solution(9945408827071738492)
XLA Ops:
  0.0 66.9 %block.1 = f32[128,384]{1,0:T(8,128)} custom-call(bf16[128,384]{1,0:T(8,128)(2,1)} %bitcast.6, s32[8,16]{1,0:T(8,128)} %tissue.1, bf16[384,1536]{1,0:T(8,128)(2,1)} %w_in.1, f32[3,3,768]{2,1,0:T(4,128)} %w_conv.1, f32[768]{0:T(1024)} %bias.1, f32[768]{0:T(1024)} %skip.1, f32[768]{0:T(1024)} %gain.1, bf16[224,768]{1,0:T(8,128)(2,1)} %bitcast.4, ...), custom_call_target="tpu_custom_call" | custom-call | tf_op jit(solution)/shard_map/block/pallas_call | solution.py:383
  67.0 1.6 %convert_element_type.3 = bf16[128,384]{1,0:T(8,128)(2,1)} convert(f32[128,384]{1,0:T(8,128)} %block.1) | non-fusion elementwise | flops 49152 | bytes 294912 | tf_op jit(solution)/shard_map/convert_element_type | solution.py:392

commit v5 on v4

--- a/solution.py
+++ b/solution.py
@@ -226,7 +226,7 @@
         return tuple(fresh), total if outputs else total + dt
 
     start = 0 if outputs else jnp.zeros((chains, width), jnp.float32)
-    return lax.fori_loop(0, steps, one, (tuple(states), start), unroll=8)
+    return lax.fori_loop(0, steps, one, (tuple(states), start), unroll=16)
 
 
 def shifted(values, by, backward):

time: 68.7 us -> 69.5 us (1.012)
  Pallas kernels: 66.9 us -> 67.7 us
    pallas_call x1, Pallas kernels: 66.9 us -> 67.7 us  [per_device(): pl.pallas_call(functools.partial(kernel, dims, specs), out_shape=jax.Shap...]
where the time goes in v5:
time: 69.5 us; the launch traced here: 69.3 us
  Pallas kernels  67.7 us (97%)
  other arithmetic  1.58 us (2%)
    pallas_call x1, Pallas kernels, per_device(): pl.pallas_call(functools.partial(kernel, dims, specs), out_shape=jax.Shap...  67.7 us
    convert_element_type x1, other arithmetic, per_device(): return out.astype(bf).reshape(rows, cols, channels)  1.58 us

profile of v5, /device:TPU:0, one launch (start us, length us, event | category | flops | bytes accessed | tf_op | source)
XLA Modules:
  0.0 69.3 jit_solution(15390045317932523370)
XLA Ops:
  0.0 67.7 %block.1 = f32[128,384]{1,0:T(8,128)} custom-call(bf16[128,384]{1,0:T(8,128)(2,1)} %bitcast.6, s32[8,16]{1,0:T(8,128)} %tissue.1, bf16[384,1536]{1,0:T(8,128)(2,1)} %w_in.1, f32[3,3,768]{2,1,0:T(4,128)} %w_conv.1, f32[768]{0:T(1024)} %bias.1, f32[768]{0:T(1024)} %skip.1, f32[768]{0:T(1024)} %gain.1, bf16[224,768]{1,0:T(8,128)(2,1)} %bitcast.4, ...), custom_call_target="tpu_custom_call" | custom-call | tf_op jit(solution)/shard_map/block/pallas_call | solution.py:383
  67.8 1.6 %convert_element_type.3 = bf16[128,384]{1,0:T(8,128)(2,1)} convert(f32[128,384]{1,0:T(8,128)} %block.1) | non-fusion elementwise | flops 49152 | bytes 294912 | tf_op jit(solution)/shard_map/convert_element_type | solution.py:392
